TPU v7x, 32 devices: a whole 2x2x4 slice. The times are simulated.
32 devices in a mesh: dp: 4 (over z), row: 2 (over y), col: 4 (over x, core).
Axes of the slice: x: 2, y: 2, z: 4, core: 2. Of those that a mesh axis runs over, the one named last changes fastest.
Arguments:
- grad_blocks: bfloat16 [4, 4096, 1024], P('dp', 'row', 'col'), may hold values from -300 to 300
- ln_grads: bfloat16 [4, 4, 1024], P('dp', None, 'col'), may hold values from -240 to 240, as said below
- master: float32 [4096, 1024], P(('row', 'col')), may hold values from -6 to 6
- first_moment: float32 [4096, 1024], P(('row', 'col')), may hold values from -6 to 6
- second_moment: float32 [4096, 1024], P(('row', 'col')), may hold values from 0.3 to 3
- average: float32 [4096, 1024], P('row', 'col'), may hold values from -6 to 6
- ln_master: float32 [4, 1024], P(None, 'col'), may hold values from -6 to 6
- ln_first: float32 [4, 1024], P(None, 'col'), may hold values from -6 to 6
- ln_second: float32 [4, 1024], P(None, 'col'), may hold values from 0.3 to 3
- ln_average: float32 [4, 1024], P(None, 'col'), may hold values from -6 to 6
Outputs:
- average_new: float32 [4096, 1024], P('row', 'col')
- master_new: float32 [4096, 1024], P(('row', 'col'))
- first_new: float32 [4096, 1024], P(('row', 'col'))
- second_new: float32 [4096, 1024], P(('row', 'col'))
- ln_master_new: float32 [4, 1024], P(None, 'col')
- ln_first_new: float32 [4, 1024], P(None, 'col')
- ln_second_new: float32 [4, 1024], P(None, 'col')
- ln_average_new: float32 [4, 1024], P(None, 'col')
Inputs may be any that keep to these rules, and one draw needn't show every extreme that they name: `ln_grads`: partial gradients of each data-parallel group.
All inputs are finite; a program needn't handle non-finite values.
Results may differ from a plain program's by a relative error of at most 0.0003.
Values may be sent and summed in bfloat16 or wider, within the bound.
No kernel may reach another device: no remote copies, remote signals or barrier semaphores. Data moves between devices by JAX's collectives and lax.ppermute only.
A program may use at most 64 MiB of HBM per device.

v0:
```python
import functools
import math

import jax
import jax.numpy as jnp
from jax import lax
from jax.experimental import pallas as pl
from jax.experimental.pallas import tpu as pltpu
from jax.sharding import PartitionSpec as P

D = 1024
FF = 4096
STEP = 20


beta_one = 0.9
beta_two = 0.95
learn_rate = 0.02
decay_rate = 0.1
epsilon = 1e-08
clip_rms = 1.0
ema_keep = 0.9


root_gain = 1.0 / math.sqrt(1.0 - beta_two**STEP)
step_gain = learn_rate / (1.0 - beta_one**STEP) / root_gain


def adam_step(gradient, clip_scale, first, second, master, decay_weight):
    clipped = clip_scale * gradient
    first_new = beta_one * first + (1.0 - beta_one) * clipped
    second_new = beta_two * second + (1.0 - beta_two) * clipped * clipped
    root = second_new * lax.rsqrt(second_new)
    step = step_gain * first_new / (root + epsilon / root_gain)
    master_new = (1.0 - learn_rate * decay_weight) * master - step
    return (master_new, first_new, second_new)


def clip_factor(norm_total):
    return jnp.minimum(1.0, clip_rms * math.sqrt(FF * D + 4 * D) / jnp.sqrt(norm_total))


def arrange(blocks, extra):
    groups, cols = lax.axis_size("dp"), lax.axis_size("col")
    _, rows, width = blocks.shape
    span = cols * rows

    def body(blocks_ref, extra_ref, *outs):
        outs[groups][...] = jnp.zeros_like(outs[groups])
        group, col = lax.axis_index("dp"), lax.axis_index("col")
        for s in range(groups):
            for k in range(cols):
                outs[s][k * rows : (k + 1) * rows] = blocks_ref[
                    (col ^ k) * groups + (group ^ s)
                ]
            outs[s][span:] = extra_ref[...]

    return pl.pallas_call(
        body,
        in_specs=[pl.BlockSpec(memory_space=pltpu.VMEM)] * 2,
        out_specs=[pl.BlockSpec(memory_space=pltpu.VMEM)] * (groups + 1),
        out_shape=[
            jax.ShapeDtypeStruct((span + extra.shape[0], width), blocks.dtype)
        ]
        * groups
        + [jax.ShapeDtypeStruct((8, 128), jnp.float32)],
        compiler_params=pltpu.CompilerParams(vmem_limit_bytes=16 * 2**20),
        name="arrange",
    )(blocks, extra)


def by_column(states, cols, after):
    rows, columns = states[0].shape
    width = columns // cols
    count = len(states)

    def body(*refs):
        for i in range(count):
            refs[count + 1][0, i] = refs[i][...]

    return pl.pallas_call(
        body,
        grid=(cols,),
        in_specs=[pl.BlockSpec((rows, width), lambda c: (0, c))] * count
        + [pl.BlockSpec(after.shape, lambda c: (0, 0))],
        out_specs=pl.BlockSpec((1, count, rows, width), lambda c: (c, 0, 0, 0)),
        out_shape=jax.ShapeDtypeStruct((cols, count, rows, width), states[0].dtype),
        compiler_params=pltpu.CompilerParams(vmem_limit_bytes=16 * 2**20),
        name="by_column",
    )(*(pltpu.with_memory_space_constraint(x, pltpu.HBM) for x in states), after)


def hand_on(norm):
    def body(norm_ref, out_ref):
        out_ref[...] = norm_ref[...]

    return pl.pallas_call(
        body,
        out_shape=jax.ShapeDtypeStruct(norm.shape, norm.dtype),
        cost_estimate=pl.CostEstimate(
            flops=0, bytes_accessed=60000000, transcendentals=0
        ),
        name="hand_on",
    )(norm)


def clip_of(norm_ref):
    rows = jnp.sum(norm_ref[...], axis=0, keepdims=True)
    return clip_factor(jnp.sum(rows, axis=1, keepdims=True))


def flat_update(place, norm, start, gradient, states, kept=(), ln_states=()):
    count, cols, rows, width = gradient.shape
    state = pl.BlockSpec(
        (rows, cols * width), lambda s, place: (place[0] ^ (start + s), 0)
    )
    whole = pl.BlockSpec(norm.shape, lambda s, place: (0, 0))
    ln = [pl.BlockSpec(x.shape, lambda s, place: (0, 0)) for x in ln_states]

    def body(place_ref, norm_ref, gradient_ref, *refs):
        refs = list(refs)
        take = lambda number: [refs.pop(0) for _ in range(number)]
        state_refs, _, ln_refs = take(3), take(len(kept)), take(len(ln))
        out_refs, passed_ref, ln_out_refs = take(3), take(1)[0], refs
        passed_ref[...] = norm_ref[...]
        clip_scale = clip_of(norm_ref)
        for column in range(cols):
            here = slice(column * width, (column + 1) * width)
            master, first, second = (ref[:, here] for ref in state_refs)
            results = adam_step(
                gradient_ref[0, place_ref[1] ^ column],
                clip_scale,
                first,
                second,
                master,
                decay_rate,
            )
            for out_ref, result in zip(out_refs, results):
                out_ref[:, here] = result

        if ln:

            @pl.when(pl.program_id(0) == 0)
            def _():
                ln_gradient, ln_master, ln_first, ln_second, ln_average = (
                    ref[...] for ref in ln_refs
                )
                results = adam_step(
                    ln_gradient, clip_scale, ln_first, ln_second, ln_master, 0.0
                )
                average = ema_keep * ln_average + (1.0 - ema_keep) * results[0]
                for out_ref, result in zip(ln_out_refs, (*results, average)):
                    out_ref[...] = result

    out = pl.pallas_call(
        body,
        grid_spec=pltpu.PrefetchScalarGridSpec(
            num_scalar_prefetch=1,
            grid=(count,),
            in_specs=[
                whole,
                pl.BlockSpec((1, cols, rows, width), lambda s, place: (s, 0, 0, 0)),
            ]
            + [state] * 3
            + [pl.BlockSpec(memory_space=pl.ANY)] * len(kept)
            + ln,
            out_specs=[state] * 3 + [whole] + ln[1:],
        ),
        out_shape=[
            jax.ShapeDtypeStruct(x.shape, x.dtype)
            for x in (*states, norm, *ln_states[1:])
        ],
        input_output_aliases={6 + i: i for i in range(len(kept))},
        compiler_params=pltpu.CompilerParams(vmem_limit_bytes=16 * 2**20),
        name="flat_update",
    )(place, norm, gradient, *states, *kept, *ln_states)
    return out[:3], out[3], out[4:]


def block_average(place, norm, gradient, states, average):
    groups, cols, rows, width = gradient.shape
    span = groups * rows

    def body(
        place_ref, norm_ref, gradient_ref, states_ref, average_ref, out_ref, passed_ref
    ):
        passed_ref[...] = norm_ref[...]
        clip_scale = clip_of(norm_ref)
        for group in range(groups):
            here = slice(group * rows, (group + 1) * rows)
            master, first, second = (states_ref[0, i, here] for i in range(3))
            master_new, _, _ = adam_step(
                gradient_ref[place_ref[0] ^ group, 0],
                clip_scale,
                first,
                second,
                master,
                decay_rate,
            )
            out_ref[here] = (
                ema_keep * average_ref[here] + (1.0 - ema_keep) * master_new
            )

    block = pl.BlockSpec((span, width), lambda c, place: (c, 0))
    return pl.pallas_call(
        body,
        grid_spec=pltpu.PrefetchScalarGridSpec(
            num_scalar_prefetch=1,
            grid=(cols,),
            in_specs=[
                pl.BlockSpec(norm.shape, lambda c, place: (0, 0)),
                pl.BlockSpec(
                    (groups, 1, rows, width),
                    lambda c, place: (0, place[1] ^ c, 0, 0),
                ),
                pl.BlockSpec((1, 3, span, width), lambda c, place: (c, 0, 0, 0)),
                block,
            ],
            out_specs=[block, pl.BlockSpec(norm.shape, lambda c, place: (0, 0))],
        ),
        out_shape=[
            jax.ShapeDtypeStruct(x.shape, x.dtype) for x in (average, norm)
        ],
        compiler_params=pltpu.CompilerParams(vmem_limit_bytes=16 * 2**20),
        name="block_average",
    )(place, norm, gradient, states, average)


def tree_sum(terms):
    while len(terms) > 1:
        terms = [a + b for a, b in zip(terms[::2], terms[1::2])]
    return terms[0]


def send(held, axis, s):
    if s == 0:
        return held
    size = lax.axis_size(axis)
    return lax.ppermute(held, axis, [(i, i ^ s) for i in range(size)])


def exchange(held, axis):
    return [send(held, axis, s) for s in range(lax.axis_size(axis))]


def shards(
    grad_blocks,
    ln_grads,
    master,
    first_moment,
    second_moment,
    average,
    ln_master,
    ln_first,
    ln_second,
    ln_average,
):
    groups, row_count, cols = (lax.axis_size(name) for name in ("dp", "row", "col"))
    place = jnp.stack([lax.axis_index("dp"), lax.axis_index("col")]).astype(jnp.int32)
    _, rows, width = grad_blocks.shape
    flat = rows // cols
    piece_rows = flat // groups
    f32, f16 = jnp.float32, jnp.float16
    states = (master, first_moment, second_moment)

    ln_rows = ln_grads.shape[1]
    *parts, after = arrange(
        grad_blocks.reshape(cols * groups, piece_rows, width),
        jnp.pad(ln_grads[0], ((0, -ln_rows % 16), (0, 0))),
    )
    parts = [send(part, "dp", s) for s, part in enumerate(parts)]

    block_states = lax.all_to_all(
        by_column(states, cols, after).astype(f16),
        "col",
        split_axis=0,
        concat_axis=0,
        tiled=True,
    )

    total = tree_sum([part.astype(f32) for part in parts])
    ln_gradient = total[cols * piece_rows :][:ln_rows]
    total = total[: cols * piece_rows].reshape(cols, piece_rows, width)
    norm = jnp.sum(total * total, axis=(0, 1)) + jnp.sum(
        ln_gradient * ln_gradient, axis=0
    ) / float(row_count * groups)
    norm = tree_sum(exchange(norm.reshape(1, width), "dp"))
    pieces = exchange(total.astype(f16), "dp")
    norm = lax.all_gather(hand_on(norm), ("row", "col"), tiled=True)

    half = groups // 2
    near = [send(jnp.stack([x[k] for x in pieces]), "col", k) for k in range(2)]
    halves = [
        [x[at] for x in near]
        + [
            send(jnp.stack([x[k] for x in pieces[at]]), "col", k)
            for k in range(2, cols)
        ]
        for at in (slice(0, half), slice(half, groups))
    ]
    average_new, norm = block_average(
        place, norm, jnp.stack(pieces).astype(f32), block_states.astype(f32), average
    )
    updated, norm, ln_updated = flat_update(
        place,
        norm,
        0,
        jnp.stack(halves[0], axis=1).astype(f32) + 0.0 * norm[:1],
        states,
        ln_states=(ln_gradient, ln_master, ln_first, ln_second, ln_average),
    )
    updated, _, _ = flat_update(
        place,
        norm,
        half,
        jnp.stack(halves[1], axis=1).astype(f32),
        states,
        updated,
    )
    return (average_new, *updated, *ln_updated)


def solution(mesh):
    placed = (
        P("dp", "row", "col"),
        P("dp", None, "col"),
        P(("row", "col"), None),
        P(("row", "col"), None),
        P(("row", "col"), None),
        P("row", "col"),
        P(None, "col"),
        P(None, "col"),
        P(None, "col"),
        P(None, "col"),
    )
    return jax.shard_map(
        shards,
        mesh=mesh,
        in_specs=placed,
        out_specs=(
            P("row", "col"),
            P(("row", "col"), None),
            P(("row", "col"), None),
            P(("row", "col"), None),
            P(None, "col"),
            P(None, "col"),
            P(None, "col"),
            P(None, "col"),
        ),
        check_vma=False,
    )
```

profile of v0, /device:TPU:0, one launch (start us, length us, event | category | flops | bytes accessed | tf_op | source)
XLA Modules:
  0.0 80.9 jit_solution(17006636265020148923)
XLA Ops:
  0.6 0.7 pad.4.extra_ref
  1.3 1.2 %copy-done.4 = bf16[1,2048,256]{2,1,0:T(8,128)(2,1)S(1)} copy-done((bf16[1,2048,256]{2,1,0:T(8,128)(2,1)S(1)}, bf16[1,2048,256]{2,1,0:T(8,128)(2,1)}, u32[]{:S(2)}) %copy-start.4) | copy-done | bytes 1048600
  2.5 0.1 arrange.1
  2.6 3.1 %collective-permute-start = (bf16[528,256]{1,0:T(8,128)(2,1)S(1)}, bf16[528,256]{1,0:T(8,128)(2,1)S(1)}, u32[]{:S(2)}, u32[]{:S(2)}) collective-permute-start(bf16[528,256]{1,0:T(8,128)(2,1)S(1)} %get-tuple-element.27), channel_id=1, source_target_pairs={{0,8},{8,0},{16,24},{24,16},{1,9},{9,1},{17,25},{25,17},{2,10},{10... | collective-permute-start | bytes 811016 | tf_op jit(solution)/shard_map/ppermute | solution.py:239
  5.7 2.6 %collective-permute-start.1 = (bf16[528,256]{1,0:T(8,128)(2,1)S(1)}, bf16[528,256]{1,0:T(8,128)(2,1)S(1)}, u32[]{:S(2)}, u32[]{:S(2)}) collective-permute-start(bf16[528,256]{1,0:T(8,128)(2,1)S(1)} %get-tuple-element.28), channel_id=1, source_target_pairs={{0,16},{8,24},{16,0},{24,8},{1,17},{9,25},{17,1},{25,9},{2,18},{10... | collective-permute-start | bytes 811016 | tf_op jit(solution)/shard_map/ppermute | solution.py:239
  8.3 3.5 %by_column.1 = f32[4,3,512,256]{3,2,1,0:T(8,128)S(1)} custom-call(f32[512,1024]{1,0:T(8,128)} %refs_0_.5, f32[512,1024]{1,0:T(8,128)} %refs_1_.5, f32[512,1024]{1,0:T(8,128)} %refs_2_.5, f32[8,128]{1,0:T(8,128)S(1)} %get-tuple-element.30.refs_3_), custom_call_target="tpu_custom_call" | custom-call | tf_op jit(solution)/shard_map/by_column/pallas_call | solution.py:81
  11.9 2.1 %convert_element_type.53 = f16[4,3,512,256]{3,2,1,0:T(8,128)(2,1)} convert(f32[4,3,512,256]{3,2,1,0:T(8,128)S(1)} %by_column.1) | non-fusion elementwise | flops 1572864 | bytes 9437184 | tf_op jit(solution)/shard_map/convert_element_type | solution.py:274
  14.0 4.7 %all-to-all-start = ((f16[4,3,512,256]{3,2,1,0:T(8,128)(2,1)}), f16[4,3,512,256]{3,2,1,0:T(8,128)(2,1)}, u32[]{:S(2)}, u32[]{:S(2)}) async-start(f16[4,3,512,256]{3,2,1,0:T(8,128)(2,1)} %convert_element_type.53), calls=%async_computation | async-start | bytes 6291456 | tf_op jit(solution)/shard_map/all_to_all | solution.py:273
  18.6 0.1 pad_add_fusion.place_ref
  18.7 0.0 collective-permute-done
  18.7 8.9 %collective-permute-done.1 = bf16[528,256]{1,0:T(8,128)(2,1)S(1)} collective-permute-done((bf16[528,256]{1,0:T(8,128)(2,1)S(1)}, bf16[528,256]{1,0:T(8,128)(2,1)S(1)}, u32[]{:S(2)}, u32[]{:S(2)}) %collective-permute-start.1) | collective-permute-done | bytes 270368 | tf_op jit(solution)/shard_map/ppermute | solution.py:239
  27.6 0.1 add_add_fusion
  27.8 0.1 slice_convert_fusion
  27.9 2.5 %collective-permute-start.5 = (f32[1,256]{1,0:T(1,128)S(1)}, f32[1,256]{1,0:T(1,128)S(1)}, u32[]{:S(2)}, u32[]{:S(2)}) collective-permute-start(f32[1,256]{1,0:T(1,128)S(1)} %bitcast.52), channel_id=1, source_target_pairs={{0,24},{8,16},{16,8},{24,0},{1,25},{9,17},{17,9},{25,1},{2,26},{10... | collective-permute-start | bytes 3080 | tf_op jit(solution)/shard_map/ppermute | solution.py:239
  30.4 3.9 %collective-permute-start.4 = (f32[1,256]{1,0:T(1,128)S(1)}, f32[1,256]{1,0:T(1,128)S(1)}, u32[]{:S(2)}, u32[]{:S(2)}) collective-permute-start(f32[1,256]{1,0:T(1,128)S(1)} %bitcast.53), channel_id=1, source_target_pairs={{0,16},{8,24},{16,0},{24,8},{1,17},{9,25},{17,1},{25,9},{2,18},{10... | collective-permute-start | bytes 3080 | tf_op jit(solution)/shard_map/ppermute | solution.py:239
  34.3 0.1 collective-permute-start.3
  34.4 2.4 %collective-permute-start.8 = (f16[4,128,256]{2,1,0:T(8,128)(2,1)S(1)}, f16[4,128,256]{2,1,0:T(8,128)(2,1)S(1)}, u32[]{:S(2)}, u32[]{:S(2)}) collective-permute-start(f16[4,128,256]{2,1,0:T(8,128)(2,1)S(1)} %bitcast.43), channel_id=1, source_target_pairs={{0,24},{8,16},{16,8},{24,0},{1,25},{9,17},{17,9},{25,1},{2,26},{10... | collective-permute-start | bytes 786440 | tf_op jit(solution)/shard_map/ppermute | solution.py:239
  36.9 1.1 %collective-permute-start.7 = (f16[4,128,256]{2,1,0:T(8,128)(2,1)S(1)}, f16[4,128,256]{2,1,0:T(8,128)(2,1)S(1)}, u32[]{:S(2)}, u32[]{:S(2)}) collective-permute-start(f16[4,128,256]{2,1,0:T(8,128)(2,1)S(1)} %bitcast.44), channel_id=1, source_target_pairs={{0,16},{8,24},{16,0},{24,8},{1,17},{9,25},{17,1},{25,9},{2,18},{10... | collective-permute-start | bytes 786440 | tf_op jit(solution)/shard_map/ppermute | solution.py:239
  37.9 0.0 collective-permute-done.5
  37.9 1.0 %collective-permute-start.6 = (f16[4,128,256]{2,1,0:T(8,128)(2,1)S(1)}, f16[4,128,256]{2,1,0:T(8,128)(2,1)S(1)}, u32[]{:S(2)}, u32[]{:S(2)}) collective-permute-start(f16[4,128,256]{2,1,0:T(8,128)(2,1)S(1)} %bitcast.45), channel_id=1, source_target_pairs={{0,8},{8,0},{16,24},{24,16},{1,9},{9,1},{17,25},{25,17},{2,10},{10... | collective-permute-start | bytes 786440 | tf_op jit(solution)/shard_map/ppermute | solution.py:239
  39.0 0.6 add_add_fusion.1.norm_ref
  39.5 1.2 %hand_on.1 = f32[1,256]{1,0:T(1,128)} custom-call(f32[1,256]{1,0:T(1,128)} %add_add_fusion.1.norm_ref), custom_call_target="tpu_custom_call" | custom-call | bytes 60000000 | tf_op jit(solution)/shard_map/hand_on/pallas_call | solution.py:97
  40.8 17.6 %all-gather = f32[8,1,256]{2,1,0:T(1,128)S(1)} all-gather(f32[1,1,256]{2,1,0:T(1,128)} %bitcast.56), channel_id=1, replica_groups=mesh['dp'=4,'row'=2,'col'=4] {'row','col'}, dimensions={0}, use_global_device_ids=true | all-gather | bytes 9216 | tf_op jit(solution)/shard_map/all_gather | solution.py:289
  58.5 0.4 collective-permute-done.7
  58.9 1.6 %collective-permute-start.12 = (f16[2,128,256]{2,1,0:T(8,128)(2,1)S(1)}, f16[2,128,256]{2,1,0:T(8,128)(2,1)S(1)}, u32[]{:S(2)}, u32[]{:S(2)}) collective-permute-start(f16[2,128,256]{2,1,0:T(8,128)(2,1)S(1)} %pad_maximum_fusion.3), channel_id=1, source_target_pairs={{0,2},{1,3},{2,0},{3,1},{4,6},{5,7},{6,4},{7,5},{8,10},{9,11},{10,... | collective-permute-start | bytes 393224 | tf_op jit(solution)/shard_map/ppermute | solution.py:239
  60.5 0.1 collective-permute-start.13
  60.6 0.0 collective-permute-done.6
  60.6 0.1 fusion.3
  60.7 1.5 %collective-permute-start.10 = (f16[2,128,256]{2,1,0:T(8,128)(2,1)S(1)}, f16[2,128,256]{2,1,0:T(8,128)(2,1)}, u32[]{:S(2)}, u32[]{:S(2)}) collective-permute-start(f16[2,128,256]{2,1,0:T(8,128)(2,1)S(1)} %pad_maximum_fusion.1), channel_id=1, source_target_pairs={{0,2},{1,3},{2,0},{3,1},{4,6},{5,7},{6,4},{7,5},{8,10},{9,11},{10,... | collective-permute-start | bytes 393224 | tf_op jit(solution)/shard_map/ppermute | solution.py:239
  62.3 0.7 pad_maximum_fusion.2
  62.9 0.5 collective-permute-start.11
  63.4 0.1 pad_maximum_fusion
  63.5 0.2 collective-permute-start.9
  63.8 0.3 maximum_convert_fusion.gradient_ref
  64.1 1.0 %collective-permute-done.9 = f16[4,128,256]{2,1,0:T(8,128)(2,1)S(1)} collective-permute-done((f16[4,128,256]{2,1,0:T(8,128)(2,1)S(1)}, f16[4,128,256]{2,1,0:T(8,128)(2,1)S(1)}, u32[]{:S(2)}, u32[]{:S(2)}) %collective-permute-start.9) | collective-permute-done | bytes 262176 | tf_op jit(solution)/shard_map/ppermute | solution.py:239
  65.2 2.0 %collective-permute-done.13 = f16[2,128,256]{2,1,0:T(8,128)(2,1)S(1)} collective-permute-done((f16[2,128,256]{2,1,0:T(8,128)(2,1)S(1)}, f16[2,128,256]{2,1,0:T(8,128)(2,1)S(1)}, u32[]{:S(2)}, u32[]{:S(2)}) %collective-permute-start.13) | collective-permute-done | bytes 131104 | tf_op jit(solution)/shard_map/ppermute | solution.py:239
  67.1 0.1 maximum_convert_fusion.1.gradient_ref
  67.3 0.0 copy-start.3
  67.3 2.6 %convert_element_type.54.states_ref = f32[4,3,512,256]{3,2,1,0:T(8,128)S(1)} convert(f16[4,3,512,256]{3,2,1,0:T(8,128)(2,1)} %all-to-all-done) | non-fusion elementwise | flops 1572864 | bytes 9437184 | tf_op jit(solution)/shard_map/convert_element_type | solution.py:302
  69.9 0.0 copy-start.1
  69.9 0.0 copy-start.2
  69.9 3.9 %block_average.1 = (f32[2048,256]{1,0:T(8,128)}, f32[8,256]{1,0:T(8,128)S(1)}) custom-call(s32[2]{0:T(128)S(1)} %pad_add_fusion.place_ref, f32[8,256]{1,0:T(8,128)S(1)} %bitcast.42, f32[4,4,128,256]{3,2,1,0:T(8,128)S(1)} %maximum_convert_fusion.gradient_ref, f32[4,3,512,256]{3,2,1,0:T(8,128)S(1)} %convert_element_type.54.states_ref, f32[2048,256]{1,0:T(8,128)S(1)} %copy-done.3), custom_call_target="tpu_custom_call" | custom-call | tf_op jit(solution)/shard_map/block_average/pallas_call | solution.py:205
  73.9 0.0 copy-start.8
  73.9 1.3 %convert_add_fusion = f32[2,4,128,256]{3,2,0,1:T(8,128)S(1)} fusion(f16[2,1,128,256]{3,2,0,1:T(8,128)(2,1)} %bitcast.18, f16[2,1,128,256]{3,2,0,1:T(8,128)(2,1)} %bitcast.16, f16[2,1,128,256]{3,2,0,1:T(8,128)(2,1)S(1)} %get-tuple-element.57, f16[2,1,128,256]{3,2,0,1:T(8,128)(2,1)S(1)} %maximum_bitcast_fusion, f32[256]{0:T(256)S(1)} %bitcast.57), kind=kLoop, calls=%fused_computation.1 | loop fusion | flops 1310720 | bytes 1573888 | tf_op jit(solution)/shard_map/add | solution.py:308
  75.2 0.1 copy.25.gradient_ref
  75.3 0.3 copy-done
  75.6 2.8 %flat_update.2 = (f32[512,1024]{1,0:T(8,128)}, f32[512,1024]{1,0:T(8,128)}, f32[512,1024]{1,0:T(8,128)}, f32[8,256]{1,0:T(8,128)S(1)}, f32[4,256]{1,0:T(4,128)},...) custom-call(s32[2]{0:T(128)S(1)} %pad_add_fusion.place_ref, f32[8,256]{1,0:T(8,128)S(1)} %get-tuple-element.32.norm_ref, ...), custom_call_target="tpu_custom_call" | custom-call | tf_op jit(solution)/shard_map/flat_update/pallas_call | solution.py:155
  78.4 2.5 %flat_update.3 = (f32[512,1024]{1,0:T(8,128)}, f32[512,1024]{1,0:T(8,128)}, f32[512,1024]{1,0:T(8,128)}, f32[8,256]{1,0:T(8,128)}) custom-call(s32[2]{0:T(128)S(1)} %pad_add_fusion.place_ref, f32[8,256]{1,0:T(8,128)S(1)} %get-tuple-element.33.norm_ref, ...), custom_call_target="tpu_custom_call", output_to_operand_aliasing={{0}: (6, {}), {1}: (7, {}), {2}: (8, {})} | custom-call | tf_op jit(solution)/shard_map/flat_update/pallas_call | solution.py:155
  (34 shorter events, 0.4 us)
Async XLA Ops:
  1.3 1.2 %copy-start.4 = (bf16[1,2048,256]{2,1,0:T(8,128)(2,1)S(1)}, bf16[1,2048,256]{2,1,0:T(8,128)(2,1)}, u32[]{:S(2)}) copy-start(bf16[1,2048,256]{2,1,0:T(8,128)(2,1)} %param.10) | copy-start | bytes 3145732
  2.6 16.1 %collective-permute-start = (bf16[528,256]{1,0:T(8,128)(2,1)S(1)}, bf16[528,256]{1,0:T(8,128)(2,1)S(1)}, u32[]{:S(2)}, u32[]{:S(2)}) collective-permute-start(bf16[528,256]{1,0:T(8,128)(2,1)S(1)} %get-tuple-element.27), channel_id=1, source_target_pairs={{0,8},{8,0},{16,24},{24,16},{1,9},{9,1},{17,25},{25,17},{2,10},{10... | collective-permute-start | bytes 811016 | tf_op jit(solution)/shard_map/ppermute | solution.py:239
  5.7 21.9 %collective-permute-start.1 = (bf16[528,256]{1,0:T(8,128)(2,1)S(1)}, bf16[528,256]{1,0:T(8,128)(2,1)S(1)}, u32[]{:S(2)}, u32[]{:S(2)}) collective-permute-start(bf16[528,256]{1,0:T(8,128)(2,1)S(1)} %get-tuple-element.28), channel_id=1, source_target_pairs={{0,16},{8,24},{16,0},{24,8},{1,17},{9,25},{17,1},{25,9},{2,18},{10... | collective-permute-start | bytes 811016 | tf_op jit(solution)/shard_map/ppermute | solution.py:239
  8.3 19.3 %collective-permute-start.2 = (bf16[528,256]{1,0:T(8,128)(2,1)S(1)}, bf16[528,256]{1,0:T(8,128)(2,1)S(1)}, u32[]{:S(2)}, u32[]{:S(2)}) collective-permute-start(bf16[528,256]{1,0:T(8,128)(2,1)S(1)} %get-tuple-element.29), channel_id=1, source_target_pairs={{0,24},{8,16},{16,8},{24,0},{1,25},{9,17},{17,9},{25,1},{2,26},{10... | collective-permute-start | bytes 811016 | tf_op jit(solution)/shard_map/ppermute | solution.py:239
  14.0 53.3 %all-to-all-start = ((f16[4,3,512,256]{3,2,1,0:T(8,128)(2,1)}), f16[4,3,512,256]{3,2,1,0:T(8,128)(2,1)}, u32[]{:S(2)}, u32[]{:S(2)}) async-start(f16[4,3,512,256]{3,2,1,0:T(8,128)(2,1)} %convert_element_type.53), calls=%async_computation | async-start | bytes 6291456 | tf_op jit(solution)/shard_map/all_to_all | solution.py:273
  27.9 10.1 %collective-permute-start.5 = (f32[1,256]{1,0:T(1,128)S(1)}, f32[1,256]{1,0:T(1,128)S(1)}, u32[]{:S(2)}, u32[]{:S(2)}) collective-permute-start(f32[1,256]{1,0:T(1,128)S(1)} %bitcast.52), channel_id=1, source_target_pairs={{0,24},{8,16},{16,8},{24,0},{1,25},{9,17},{17,9},{25,1},{2,26},{10... | collective-permute-start | bytes 3080 | tf_op jit(solution)/shard_map/ppermute | solution.py:239
  30.4 8.6 %collective-permute-start.4 = (f32[1,256]{1,0:T(1,128)S(1)}, f32[1,256]{1,0:T(1,128)S(1)}, u32[]{:S(2)}, u32[]{:S(2)}) collective-permute-start(f32[1,256]{1,0:T(1,128)S(1)} %bitcast.53), channel_id=1, source_target_pairs={{0,16},{8,24},{16,0},{24,8},{1,17},{9,25},{17,1},{25,9},{2,18},{10... | collective-permute-start | bytes 3080 | tf_op jit(solution)/shard_map/ppermute | solution.py:239
  34.3 4.6 %collective-permute-start.3 = (f32[1,256]{1,0:T(1,128)S(1)}, f32[1,256]{1,0:T(1,128)S(1)}, u32[]{:S(2)}, u32[]{:S(2)}) collective-permute-start(f32[1,256]{1,0:T(1,128)S(1)} %bitcast.54), channel_id=1, source_target_pairs={{0,8},{8,0},{16,24},{24,16},{1,9},{9,1},{17,25},{25,17},{2,10},{10... | collective-permute-start | bytes 3080 | tf_op jit(solution)/shard_map/ppermute | solution.py:239
  34.4 24.0 %collective-permute-start.8 = (f16[4,128,256]{2,1,0:T(8,128)(2,1)S(1)}, f16[4,128,256]{2,1,0:T(8,128)(2,1)S(1)}, u32[]{:S(2)}, u32[]{:S(2)}) collective-permute-start(f16[4,128,256]{2,1,0:T(8,128)(2,1)S(1)} %bitcast.43), channel_id=1, source_target_pairs={{0,24},{8,16},{16,8},{24,0},{1,25},{9,17},{17,9},{25,1},{2,26},{10... | collective-permute-start | bytes 786440 | tf_op jit(solution)/shard_map/ppermute | solution.py:239
  36.9 22.0 %collective-permute-start.7 = (f16[4,128,256]{2,1,0:T(8,128)(2,1)S(1)}, f16[4,128,256]{2,1,0:T(8,128)(2,1)S(1)}, u32[]{:S(2)}, u32[]{:S(2)}) collective-permute-start(f16[4,128,256]{2,1,0:T(8,128)(2,1)S(1)} %bitcast.44), channel_id=1, source_target_pairs={{0,16},{8,24},{16,0},{24,8},{1,17},{9,25},{17,1},{25,9},{2,18},{10... | collective-permute-start | bytes 786440 | tf_op jit(solution)/shard_map/ppermute | solution.py:239
  37.9 22.7 %collective-permute-start.6 = (f16[4,128,256]{2,1,0:T(8,128)(2,1)S(1)}, f16[4,128,256]{2,1,0:T(8,128)(2,1)S(1)}, u32[]{:S(2)}, u32[]{:S(2)}) collective-permute-start(f16[4,128,256]{2,1,0:T(8,128)(2,1)S(1)} %bitcast.45), channel_id=1, source_target_pairs={{0,8},{8,0},{16,24},{24,16},{1,9},{9,1},{17,25},{25,17},{2,10},{10... | collective-permute-start | bytes 786440 | tf_op jit(solution)/shard_map/ppermute | solution.py:239
  58.9 6.3 %collective-permute-start.12 = (f16[2,128,256]{2,1,0:T(8,128)(2,1)S(1)}, f16[2,128,256]{2,1,0:T(8,128)(2,1)S(1)}, u32[]{:S(2)}, u32[]{:S(2)}) collective-permute-start(f16[2,128,256]{2,1,0:T(8,128)(2,1)S(1)} %pad_maximum_fusion.3), channel_id=1, source_target_pairs={{0,2},{1,3},{2,0},{3,1},{4,6},{5,7},{6,4},{7,5},{8,10},{9,11},{10,... | collective-permute-start | bytes 393224 | tf_op jit(solution)/shard_map/ppermute | solution.py:239
  60.5 6.6 %collective-permute-start.13 = (f16[2,128,256]{2,1,0:T(8,128)(2,1)S(1)}, f16[2,128,256]{2,1,0:T(8,128)(2,1)S(1)}, u32[]{:S(2)}, u32[]{:S(2)}) collective-permute-start(f16[2,128,256]{2,1,0:T(8,128)(2,1)S(1)} %pad_maximum_fusion.4), channel_id=1, source_target_pairs={{0,3},{1,2},{2,1},{3,0},{4,7},{5,6},{6,5},{7,4},{8,11},{9,10},{10,... | collective-permute-start | bytes 393224 | tf_op jit(solution)/shard_map/ppermute | solution.py:239
  60.7 13.2 %collective-permute-start.10 = (f16[2,128,256]{2,1,0:T(8,128)(2,1)S(1)}, f16[2,128,256]{2,1,0:T(8,128)(2,1)}, u32[]{:S(2)}, u32[]{:S(2)}) collective-permute-start(f16[2,128,256]{2,1,0:T(8,128)(2,1)S(1)} %pad_maximum_fusion.1), channel_id=1, source_target_pairs={{0,2},{1,3},{2,0},{3,1},{4,6},{5,7},{6,4},{7,5},{8,10},{9,11},{10,... | collective-permute-start | bytes 393224 | tf_op jit(solution)/shard_map/ppermute | solution.py:239
  62.9 11.0 %collective-permute-start.11 = (f16[2,128,256]{2,1,0:T(8,128)(2,1)}, f16[2,128,256]{2,1,0:T(8,128)(2,1)}, u32[]{:S(2)}, u32[]{:S(2)}) collective-permute-start(f16[2,128,256]{2,1,0:T(8,128)(2,1)} %pad_maximum_fusion.2), channel_id=1, source_target_pairs={{0,3},{1,2},{2,1},{3,0},{4,7},{5,6},{6,5},{7,4},{8,11},{9,10},{10,... | collective-permute-start | bytes 393224 | tf_op jit(solution)/shard_map/ppermute | solution.py:239
  63.5 1.6 %collective-permute-start.9 = (f16[4,128,256]{2,1,0:T(8,128)(2,1)S(1)}, f16[4,128,256]{2,1,0:T(8,128)(2,1)S(1)}, u32[]{:S(2)}, u32[]{:S(2)}) collective-permute-start(f16[4,128,256]{2,1,0:T(8,128)(2,1)S(1)} %pad_maximum_fusion), channel_id=1, source_target_pairs={{0,1},{1,0},{2,3},{3,2},{4,5},{5,4},{6,7},{7,6},{8,9},{9,8},{10,11... | collective-permute-start | bytes 786440 | tf_op jit(solution)/shard_map/ppermute | solution.py:239
  67.3 2.6 %copy-start.3 = (f32[2048,256]{1,0:T(8,128)S(1)}, f32[2048,256]{1,0:T(8,128)}, u32[]{:S(2)}) copy-start(f32[2048,256]{1,0:T(8,128)} %average_ref.1) | copy-start | bytes 6291460
  69.9 5.4 %copy-start.1 = (f32[512,1024]{1,0:T(8,128)S(1)}, f32[512,1024]{1,0:T(8,128)}, u32[]{:S(2)}) copy-start(f32[512,1024]{1,0:T(8,128)} %refs_1_.5) | copy-start | bytes 6291460
  69.9 5.4 %copy-start.2 = (f32[512,1024]{1,0:T(8,128)S(1)}, f32[512,1024]{1,0:T(8,128)}, u32[]{:S(2)}) copy-start(f32[512,1024]{1,0:T(8,128)} %refs_2_.5) | copy-start | bytes 6291460
  73.9 1.7 %copy-start = (f32[512,1024]{1,0:T(8,128)S(1)}, f32[512,1024]{1,0:T(8,128)}, u32[]{:S(2)}) copy-start(f32[512,1024]{1,0:T(8,128)} %refs_0_.5) | copy-start | bytes 6291460
  73.9 1.7 %copy-start.5 = (f32[4,256]{1,0:T(4,128)S(1)}, f32[4,256]{1,0:T(4,128)}, u32[]{:S(2)}) copy-start(f32[4,256]{1,0:T(4,128)} %refs_4_.1) | copy-start | bytes 12292
  73.9 1.7 %copy-start.6 = (f32[4,256]{1,0:T(4,128)S(1)}, f32[4,256]{1,0:T(4,128)}, u32[]{:S(2)}) copy-start(f32[4,256]{1,0:T(4,128)} %refs_5_.1) | copy-start | bytes 12292
  73.9 1.7 %copy-start.7 = (f32[4,256]{1,0:T(4,128)S(1)}, f32[4,256]{1,0:T(4,128)}, u32[]{:S(2)}) copy-start(f32[4,256]{1,0:T(4,128)} %refs_6_.1) | copy-start | bytes 12292
  73.9 1.7 %copy-start.8 = (f32[4,256]{1,0:T(4,128)S(1)}, f32[4,256]{1,0:T(4,128)}, u32[]{:S(2)}) copy-start(f32[4,256]{1,0:T(4,128)} %refs_7_.1) | copy-start | bytes 12292
where the time goes:
time: 81.5 us; the launch traced here: 80.9 us
  starting transfers between devices  25.3 us (31%)
  blocking collectives  17.6 us (22%)
  Pallas kernels  14.1 us (17%)
  waiting for transfers between devices  12.2 us (15%)
  other arithmetic  8.19 us (10%)
  local copies, waits for them, and re-layouts  2.57 us (3%)
  between operations  0.89 us (1%)
    ppermute x14, starting transfers between devices, send(): return lax.ppermute(held, axis, [(i, i ^ s) for i in range(size)])  20.6 us
    all_gather x1, blocking collectives, shards(): norm = lax.all_gather(hand_on(norm), ('row', 'col'), tiled=True)  17.6 us
    ppermute x14, waiting for transfers between devices, send(): return lax.ppermute(held, axis, [(i, i ^ s) for i in range(size)])  12.2 us
    pallas_call x2, Pallas kernels, flat_update(): pl.pallas_call(body, grid_spec=pltpu.PrefetchScalarGridSpec(num_scalar_pr...  5.29 us
    all_to_all x1, starting transfers between devices, shards(): lax.all_to_all(by_column(states, cols, after).astype(f16), 'col', split_a...  4.66 us
    pallas_call x1, Pallas kernels, block_average(): pl.pallas_call(body, grid_spec=pltpu.PrefetchScalarGridSpec(num_scalar_pr...  3.94 us
    pallas_call x1, Pallas kernels, by_column(): pl.pallas_call(body, grid=(cols,), in_specs=[pl.BlockSpec((rows, width),...  3.55 us
    convert_element_type x1, other arithmetic, shards(): block_states.astype(f32)  2.59 us
  transfers between devices with their start and end apart: 15, of which 4 were waited for; matrix products, arithmetic and copies ran while one was open for 9% of the time, Pallas kernels for 11%

commit v1 on v0

--- a/solution.py
+++ b/solution.py
@@ -44,23 +44,30 @@
     groups, cols = lax.axis_size("dp"), lax.axis_size("col")
     _, rows, width = blocks.shape
     span = cols * rows
+    tail = -(-extra.shape[0] // 16) * 16
 
     def body(blocks_ref, extra_ref, *outs):
         outs[groups][...] = jnp.zeros_like(outs[groups])
         group, col = lax.axis_index("dp"), lax.axis_index("col")
+        values = extra_ref[...].astype(jnp.float32)
+        row = lax.broadcasted_iota(jnp.int32, (tail, width), 0)
+        padded = jnp.zeros((tail, width), jnp.float32)
+        for at in range(values.shape[0]):
+            padded = jnp.where(row == at, values[at : at + 1], padded)
+        padded = padded.astype(blocks.dtype)
         for s in range(groups):
             for k in range(cols):
                 outs[s][k * rows : (k + 1) * rows] = blocks_ref[
                     (col ^ k) * groups + (group ^ s)
                 ]
-            outs[s][span:] = extra_ref[...]
+            outs[s][span:] = padded
 
     return pl.pallas_call(
         body,
         in_specs=[pl.BlockSpec(memory_space=pltpu.VMEM)] * 2,
         out_specs=[pl.BlockSpec(memory_space=pltpu.VMEM)] * (groups + 1),
         out_shape=[
-            jax.ShapeDtypeStruct((span + extra.shape[0], width), blocks.dtype)
+            jax.ShapeDtypeStruct((span + tail, width), blocks.dtype)
         ]
         * groups
         + [jax.ShapeDtypeStruct((8, 128), jnp.float32)],
@@ -266,7 +273,7 @@
     ln_rows = ln_grads.shape[1]
     *parts, after = arrange(
         grad_blocks.reshape(cols * groups, piece_rows, width),
-        jnp.pad(ln_grads[0], ((0, -ln_rows % 16), (0, 0))),
+        ln_grads[0],
     )
     parts = [send(part, "dp", s) for s, part in enumerate(parts)]
 

time: 81.5 us -> 81.5 us (level)
    unnamed x19 -> x21, local copies, waits for them, and re-layouts: 1.57 us -> 2.24 us
where the time goes in v1:
time: 81.5 us; the launch traced here: 80.9 us
  starting transfers between devices  25.3 us (31%)
  blocking collectives  17.6 us (22%)
  Pallas kernels  14.1 us (17%)
  waiting for transfers between devices  12.2 us (15%)
  other arithmetic  8.2 us (10%)
  local copies, waits for them, and re-layouts  2.56 us (3%)
  between operations  0.89 us (1%)
    ppermute x14, starting transfers between devices, send(): return lax.ppermute(held, axis, [(i, i ^ s) for i in range(size)])  20.6 us
    all_gather x1, blocking collectives, shards(): norm = lax.all_gather(hand_on(norm), ('row', 'col'), tiled=True)  17.6 us
    ppermute x14, waiting for transfers between devices, send(): return lax.ppermute(held, axis, [(i, i ^ s) for i in range(size)])  12.2 us
    pallas_call x2, Pallas kernels, flat_update(): pl.pallas_call(body, grid_spec=pltpu.PrefetchScalarGridSpec(num_scalar_pr...  5.29 us
    all_to_all x1, starting transfers between devices, shards(): lax.all_to_all(by_column(states, cols, after).astype(f16), 'col', split_a...  4.66 us
    pallas_call x1, Pallas kernels, block_average(): pl.pallas_call(body, grid_spec=pltpu.PrefetchScalarGridSpec(num_scalar_pr...  3.94 us
    pallas_call x1, Pallas kernels, by_column(): pl.pallas_call(body, grid=(cols,), in_specs=[pl.BlockSpec((rows, width),...  3.55 us
    convert_element_type x1, other arithmetic, shards(): block_states.astype(f32)  2.59 us
  transfers between devices with their start and end apart: 15, of which 4 were waited for; matrix products, arithmetic and copies ran while one was open for 9% of the time, Pallas kernels for 11%

profile of v1, /device:TPU:0, one launch (start us, length us, event | category | flops | bytes accessed | tf_op | source)
XLA Modules:
  0.0 80.9 jit_solution(1334896173030172072)
XLA Ops:
  0.6 1.2 %copy-done.4 = bf16[1,2048,256]{2,1,0:T(8,128)(2,1)S(1)} copy-done((bf16[1,2048,256]{2,1,0:T(8,128)(2,1)S(1)}, bf16[1,2048,256]{2,1,0:T(8,128)(2,1)}, u32[]{:S(2)}) %copy-start.4) | copy-done | bytes 1048600
  1.9 0.7 copy-done.9
  2.5 0.1 arrange.1
  2.6 3.1 %collective-permute-start = (bf16[528,256]{1,0:T(8,128)(2,1)S(1)}, bf16[528,256]{1,0:T(8,128)(2,1)S(1)}, u32[]{:S(2)}, u32[]{:S(2)}) collective-permute-start(bf16[528,256]{1,0:T(8,128)(2,1)S(1)} %get-tuple-element.27), channel_id=1, source_target_pairs={{0,8},{8,0},{16,24},{24,16},{1,9},{9,1},{17,25},{25,17},{2,10},{10... | collective-permute-start | bytes 811016 | tf_op jit(solution)/shard_map/ppermute | solution.py:246
  5.7 2.6 %collective-permute-start.1 = (bf16[528,256]{1,0:T(8,128)(2,1)S(1)}, bf16[528,256]{1,0:T(8,128)(2,1)S(1)}, u32[]{:S(2)}, u32[]{:S(2)}) collective-permute-start(bf16[528,256]{1,0:T(8,128)(2,1)S(1)} %get-tuple-element.28), channel_id=1, source_target_pairs={{0,16},{8,24},{16,0},{24,8},{1,17},{9,25},{17,1},{25,9},{2,18},{10... | collective-permute-start | bytes 811016 | tf_op jit(solution)/shard_map/ppermute | solution.py:246
  8.3 3.5 %by_column.1 = f32[4,3,512,256]{3,2,1,0:T(8,128)S(1)} custom-call(f32[512,1024]{1,0:T(8,128)} %refs_0_.5, f32[512,1024]{1,0:T(8,128)} %refs_1_.5, f32[512,1024]{1,0:T(8,128)} %refs_2_.5, f32[8,128]{1,0:T(8,128)S(1)} %get-tuple-element.30.refs_3_), custom_call_target="tpu_custom_call" | custom-call | tf_op jit(solution)/shard_map/by_column/pallas_call | solution.py:88
  11.9 2.1 %convert_element_type.51 = f16[4,3,512,256]{3,2,1,0:T(8,128)(2,1)} convert(f32[4,3,512,256]{3,2,1,0:T(8,128)S(1)} %by_column.1) | non-fusion elementwise | flops 1572864 | bytes 9437184 | tf_op jit(solution)/shard_map/convert_element_type | solution.py:281
  14.0 4.7 %all-to-all-start = ((f16[4,3,512,256]{3,2,1,0:T(8,128)(2,1)}), f16[4,3,512,256]{3,2,1,0:T(8,128)(2,1)}, u32[]{:S(2)}, u32[]{:S(2)}) async-start(f16[4,3,512,256]{3,2,1,0:T(8,128)(2,1)} %convert_element_type.51), calls=%async_computation | async-start | bytes 6291456 | tf_op jit(solution)/shard_map/all_to_all | solution.py:280
  18.6 0.1 pad_add_fusion.place_ref
  18.7 0.0 collective-permute-done
  18.7 8.9 %collective-permute-done.1 = bf16[528,256]{1,0:T(8,128)(2,1)S(1)} collective-permute-done((bf16[528,256]{1,0:T(8,128)(2,1)S(1)}, bf16[528,256]{1,0:T(8,128)(2,1)S(1)}, u32[]{:S(2)}, u32[]{:S(2)}) %collective-permute-start.1) | collective-permute-done | bytes 270368 | tf_op jit(solution)/shard_map/ppermute | solution.py:246
  27.6 0.1 add_add_fusion
  27.8 0.1 slice_convert_fusion
  27.9 2.5 %collective-permute-start.5 = (f32[1,256]{1,0:T(1,128)S(1)}, f32[1,256]{1,0:T(1,128)S(1)}, u32[]{:S(2)}, u32[]{:S(2)}) collective-permute-start(f32[1,256]{1,0:T(1,128)S(1)} %bitcast.53), channel_id=1, source_target_pairs={{0,24},{8,16},{16,8},{24,0},{1,25},{9,17},{17,9},{25,1},{2,26},{10... | collective-permute-start | bytes 3080 | tf_op jit(solution)/shard_map/ppermute | solution.py:246
  30.4 3.9 %collective-permute-start.4 = (f32[1,256]{1,0:T(1,128)S(1)}, f32[1,256]{1,0:T(1,128)S(1)}, u32[]{:S(2)}, u32[]{:S(2)}) collective-permute-start(f32[1,256]{1,0:T(1,128)S(1)} %bitcast.54), channel_id=1, source_target_pairs={{0,16},{8,24},{16,0},{24,8},{1,17},{9,25},{17,1},{25,9},{2,18},{10... | collective-permute-start | bytes 3080 | tf_op jit(solution)/shard_map/ppermute | solution.py:246
  34.3 0.1 collective-permute-start.3
  34.4 2.4 %collective-permute-start.8 = (f16[4,128,256]{2,1,0:T(8,128)(2,1)S(1)}, f16[4,128,256]{2,1,0:T(8,128)(2,1)S(1)}, u32[]{:S(2)}, u32[]{:S(2)}) collective-permute-start(f16[4,128,256]{2,1,0:T(8,128)(2,1)S(1)} %bitcast.44), channel_id=1, source_target_pairs={{0,24},{8,16},{16,8},{24,0},{1,25},{9,17},{17,9},{25,1},{2,26},{10... | collective-permute-start | bytes 786440 | tf_op jit(solution)/shard_map/ppermute | solution.py:246
  36.9 1.1 %collective-permute-start.7 = (f16[4,128,256]{2,1,0:T(8,128)(2,1)S(1)}, f16[4,128,256]{2,1,0:T(8,128)(2,1)S(1)}, u32[]{:S(2)}, u32[]{:S(2)}) collective-permute-start(f16[4,128,256]{2,1,0:T(8,128)(2,1)S(1)} %bitcast.45), channel_id=1, source_target_pairs={{0,16},{8,24},{16,0},{24,8},{1,17},{9,25},{17,1},{25,9},{2,18},{10... | collective-permute-start | bytes 786440 | tf_op jit(solution)/shard_map/ppermute | solution.py:246
  37.9 0.0 collective-permute-done.5
  37.9 1.0 %collective-permute-start.6 = (f16[4,128,256]{2,1,0:T(8,128)(2,1)S(1)}, f16[4,128,256]{2,1,0:T(8,128)(2,1)S(1)}, u32[]{:S(2)}, u32[]{:S(2)}) collective-permute-start(f16[4,128,256]{2,1,0:T(8,128)(2,1)S(1)} %bitcast.46), channel_id=1, source_target_pairs={{0,8},{8,0},{16,24},{24,16},{1,9},{9,1},{17,25},{25,17},{2,10},{10... | collective-permute-start | bytes 786440 | tf_op jit(solution)/shard_map/ppermute | solution.py:246
  39.0 0.6 add_add_fusion.1.norm_ref
  39.5 1.2 %hand_on.1 = f32[1,256]{1,0:T(1,128)} custom-call(f32[1,256]{1,0:T(1,128)} %add_add_fusion.1.norm_ref), custom_call_target="tpu_custom_call" | custom-call | bytes 60000000 | tf_op jit(solution)/shard_map/hand_on/pallas_call | solution.py:104
  40.8 17.6 %all-gather = f32[8,1,256]{2,1,0:T(1,128)S(1)} all-gather(f32[1,1,256]{2,1,0:T(1,128)} %bitcast.57), channel_id=1, replica_groups=mesh['dp'=4,'row'=2,'col'=4] {'row','col'}, dimensions={0}, use_global_device_ids=true | all-gather | bytes 9216 | tf_op jit(solution)/shard_map/all_gather | solution.py:296
  58.5 0.3 collective-permute-done.7
  58.9 1.6 %collective-permute-start.12 = (f16[2,128,256]{2,1,0:T(8,128)(2,1)S(1)}, f16[2,128,256]{2,1,0:T(8,128)(2,1)S(1)}, u32[]{:S(2)}, u32[]{:S(2)}) collective-permute-start(f16[2,128,256]{2,1,0:T(8,128)(2,1)S(1)} %pad_maximum_fusion.3), channel_id=1, source_target_pairs={{0,2},{1,3},{2,0},{3,1},{4,6},{5,7},{6,4},{7,5},{8,10},{9,11},{10,... | collective-permute-start | bytes 393224 | tf_op jit(solution)/shard_map/ppermute | solution.py:246
  60.5 0.1 collective-permute-start.13
  60.6 0.1 fusion.3
  60.7 1.6 %collective-permute-start.10 = (f16[2,128,256]{2,1,0:T(8,128)(2,1)S(1)}, f16[2,128,256]{2,1,0:T(8,128)(2,1)}, u32[]{:S(2)}, u32[]{:S(2)}) collective-permute-start(f16[2,128,256]{2,1,0:T(8,128)(2,1)S(1)} %pad_maximum_fusion.1), channel_id=1, source_target_pairs={{0,2},{1,3},{2,0},{3,1},{4,6},{5,7},{6,4},{7,5},{8,10},{9,11},{10,... | collective-permute-start | bytes 393224 | tf_op jit(solution)/shard_map/ppermute | solution.py:246
  62.3 0.7 pad_maximum_fusion.2
  63.0 0.5 collective-permute-start.11
  63.4 0.1 pad_maximum_fusion
  63.5 0.2 collective-permute-start.9
  63.8 0.3 maximum_convert_fusion.gradient_ref
  64.1 1.0 %collective-permute-done.9 = f16[4,128,256]{2,1,0:T(8,128)(2,1)S(1)} collective-permute-done((f16[4,128,256]{2,1,0:T(8,128)(2,1)S(1)}, f16[4,128,256]{2,1,0:T(8,128)(2,1)S(1)}, u32[]{:S(2)}, u32[]{:S(2)}) %collective-permute-start.9) | collective-permute-done | bytes 262176 | tf_op jit(solution)/shard_map/ppermute | solution.py:246
  65.2 0.0 collective-permute-done.12
  65.2 2.0 %collective-permute-done.13 = f16[2,128,256]{2,1,0:T(8,128)(2,1)S(1)} collective-permute-done((f16[2,128,256]{2,1,0:T(8,128)(2,1)S(1)}, f16[2,128,256]{2,1,0:T(8,128)(2,1)S(1)}, u32[]{:S(2)}, u32[]{:S(2)}) %collective-permute-start.13) | collective-permute-done | bytes 131104 | tf_op jit(solution)/shard_map/ppermute | solution.py:246
  67.1 0.1 maximum_convert_fusion.1.gradient_ref
  67.3 0.0 copy-start.3
  67.3 2.6 %convert_element_type.52.states_ref = f32[4,3,512,256]{3,2,1,0:T(8,128)S(1)} convert(f16[4,3,512,256]{3,2,1,0:T(8,128)(2,1)} %all-to-all-done) | non-fusion elementwise | flops 1572864 | bytes 9437184 | tf_op jit(solution)/shard_map/convert_element_type | solution.py:309
  69.9 0.0 copy-start.1
  69.9 0.0 copy-start.2
  69.9 3.9 %block_average.1 = (f32[2048,256]{1,0:T(8,128)}, f32[8,256]{1,0:T(8,128)S(1)}) custom-call(s32[2]{0:T(128)S(1)} %pad_add_fusion.place_ref, f32[8,256]{1,0:T(8,128)S(1)} %bitcast.42, f32[4,4,128,256]{3,2,1,0:T(8,128)S(1)} %maximum_convert_fusion.gradient_ref, f32[4,3,512,256]{3,2,1,0:T(8,128)S(1)} %convert_element_type.52.states_ref, f32[2048,256]{1,0:T(8,128)S(1)} %copy-done.3), custom_call_target="tpu_custom_call" | custom-call | tf_op jit(solution)/shard_map/block_average/pallas_call | solution.py:212
  73.9 0.0 copy-start.8
  73.9 1.3 %convert_add_fusion = f32[2,4,128,256]{3,2,0,1:T(8,128)S(1)} fusion(f16[2,1,128,256]{3,2,0,1:T(8,128)(2,1)} %bitcast.18, f16[2,1,128,256]{3,2,0,1:T(8,128)(2,1)} %bitcast.16, f16[2,1,128,256]{3,2,0,1:T(8,128)(2,1)S(1)} %get-tuple-element.57, f16[2,1,128,256]{3,2,0,1:T(8,128)(2,1)S(1)} %maximum_bitcast_fusion, f32[256]{0:T(256)S(1)} %bitcast.58), kind=kLoop, calls=%fused_computation.1 | loop fusion | flops 1310720 | bytes 1573888 | tf_op jit(solution)/shard_map/add | solution.py:315
  75.2 0.1 copy.25.gradient_ref
  75.3 0.3 copy-done
  75.6 2.8 %flat_update.2 = (f32[512,1024]{1,0:T(8,128)}, f32[512,1024]{1,0:T(8,128)}, f32[512,1024]{1,0:T(8,128)}, f32[8,256]{1,0:T(8,128)S(1)}, f32[4,256]{1,0:T(4,128)},...) custom-call(s32[2]{0:T(128)S(1)} %pad_add_fusion.place_ref, f32[8,256]{1,0:T(8,128)S(1)} %get-tuple-element.32.norm_ref, ...), custom_call_target="tpu_custom_call" | custom-call | tf_op jit(solution)/shard_map/flat_update/pallas_call | solution.py:162
  78.4 2.5 %flat_update.3 = (f32[512,1024]{1,0:T(8,128)}, f32[512,1024]{1,0:T(8,128)}, f32[512,1024]{1,0:T(8,128)}, f32[8,256]{1,0:T(8,128)}) custom-call(s32[2]{0:T(128)S(1)} %pad_add_fusion.place_ref, f32[8,256]{1,0:T(8,128)S(1)} %get-tuple-element.33.norm_ref, ...), custom_call_target="tpu_custom_call", output_to_operand_aliasing={{0}: (6, {}), {1}: (7, {}), {2}: (8, {})} | custom-call | tf_op jit(solution)/shard_map/flat_update/pallas_call | solution.py:162
  (35 shorter events, 0.4 us)
Async XLA Ops:
  0.6 1.2 %copy-start.4 = (bf16[1,2048,256]{2,1,0:T(8,128)(2,1)S(1)}, bf16[1,2048,256]{2,1,0:T(8,128)(2,1)}, u32[]{:S(2)}) copy-start(bf16[1,2048,256]{2,1,0:T(8,128)(2,1)} %param.10) | copy-start | bytes 3145732
  1.9 0.7 copy-start.9
  2.6 16.1 %collective-permute-start = (bf16[528,256]{1,0:T(8,128)(2,1)S(1)}, bf16[528,256]{1,0:T(8,128)(2,1)S(1)}, u32[]{:S(2)}, u32[]{:S(2)}) collective-permute-start(bf16[528,256]{1,0:T(8,128)(2,1)S(1)} %get-tuple-element.27), channel_id=1, source_target_pairs={{0,8},{8,0},{16,24},{24,16},{1,9},{9,1},{17,25},{25,17},{2,10},{10... | collective-permute-start | bytes 811016 | tf_op jit(solution)/shard_map/ppermute | solution.py:246
  5.7 21.9 %collective-permute-start.1 = (bf16[528,256]{1,0:T(8,128)(2,1)S(1)}, bf16[528,256]{1,0:T(8,128)(2,1)S(1)}, u32[]{:S(2)}, u32[]{:S(2)}) collective-permute-start(bf16[528,256]{1,0:T(8,128)(2,1)S(1)} %get-tuple-element.28), channel_id=1, source_target_pairs={{0,16},{8,24},{16,0},{24,8},{1,17},{9,25},{17,1},{25,9},{2,18},{10... | collective-permute-start | bytes 811016 | tf_op jit(solution)/shard_map/ppermute | solution.py:246
  8.3 19.3 %collective-permute-start.2 = (bf16[528,256]{1,0:T(8,128)(2,1)S(1)}, bf16[528,256]{1,0:T(8,128)(2,1)S(1)}, u32[]{:S(2)}, u32[]{:S(2)}) collective-permute-start(bf16[528,256]{1,0:T(8,128)(2,1)S(1)} %get-tuple-element.29), channel_id=1, source_target_pairs={{0,24},{8,16},{16,8},{24,0},{1,25},{9,17},{17,9},{25,1},{2,26},{10... | collective-permute-start | bytes 811016 | tf_op jit(solution)/shard_map/ppermute | solution.py:246
  14.0 53.3 %all-to-all-start = ((f16[4,3,512,256]{3,2,1,0:T(8,128)(2,1)}), f16[4,3,512,256]{3,2,1,0:T(8,128)(2,1)}, u32[]{:S(2)}, u32[]{:S(2)}) async-start(f16[4,3,512,256]{3,2,1,0:T(8,128)(2,1)} %convert_element_type.51), calls=%async_computation | async-start | bytes 6291456 | tf_op jit(solution)/shard_map/all_to_all | solution.py:280
  27.9 10.1 %collective-permute-start.5 = (f32[1,256]{1,0:T(1,128)S(1)}, f32[1,256]{1,0:T(1,128)S(1)}, u32[]{:S(2)}, u32[]{:S(2)}) collective-permute-start(f32[1,256]{1,0:T(1,128)S(1)} %bitcast.53), channel_id=1, source_target_pairs={{0,24},{8,16},{16,8},{24,0},{1,25},{9,17},{17,9},{25,1},{2,26},{10... | collective-permute-start | bytes 3080 | tf_op jit(solution)/shard_map/ppermute | solution.py:246
  30.4 8.6 %collective-permute-start.4 = (f32[1,256]{1,0:T(1,128)S(1)}, f32[1,256]{1,0:T(1,128)S(1)}, u32[]{:S(2)}, u32[]{:S(2)}) collective-permute-start(f32[1,256]{1,0:T(1,128)S(1)} %bitcast.54), channel_id=1, source_target_pairs={{0,16},{8,24},{16,0},{24,8},{1,17},{9,25},{17,1},{25,9},{2,18},{10... | collective-permute-start | bytes 3080 | tf_op jit(solution)/shard_map/ppermute | solution.py:246
  34.3 4.6 %collective-permute-start.3 = (f32[1,256]{1,0:T(1,128)S(1)}, f32[1,256]{1,0:T(1,128)S(1)}, u32[]{:S(2)}, u32[]{:S(2)}) collective-permute-start(f32[1,256]{1,0:T(1,128)S(1)} %bitcast.55), channel_id=1, source_target_pairs={{0,8},{8,0},{16,24},{24,16},{1,9},{9,1},{17,25},{25,17},{2,10},{10... | collective-permute-start | bytes 3080 | tf_op jit(solution)/shard_map/ppermute | solution.py:246
  34.4 24.0 %collective-permute-start.8 = (f16[4,128,256]{2,1,0:T(8,128)(2,1)S(1)}, f16[4,128,256]{2,1,0:T(8,128)(2,1)S(1)}, u32[]{:S(2)}, u32[]{:S(2)}) collective-permute-start(f16[4,128,256]{2,1,0:T(8,128)(2,1)S(1)} %bitcast.44), channel_id=1, source_target_pairs={{0,24},{8,16},{16,8},{24,0},{1,25},{9,17},{17,9},{25,1},{2,26},{10... | collective-permute-start | bytes 786440 | tf_op jit(solution)/shard_map/ppermute | solution.py:246
  36.9 22.0 %collective-permute-start.7 = (f16[4,128,256]{2,1,0:T(8,128)(2,1)S(1)}, f16[4,128,256]{2,1,0:T(8,128)(2,1)S(1)}, u32[]{:S(2)}, u32[]{:S(2)}) collective-permute-start(f16[4,128,256]{2,1,0:T(8,128)(2,1)S(1)} %bitcast.45), channel_id=1, source_target_pairs={{0,16},{8,24},{16,0},{24,8},{1,17},{9,25},{17,1},{25,9},{2,18},{10... | collective-permute-start | bytes 786440 | tf_op jit(solution)/shard_map/ppermute | solution.py:246
  37.9 22.7 %collective-permute-start.6 = (f16[4,128,256]{2,1,0:T(8,128)(2,1)S(1)}, f16[4,128,256]{2,1,0:T(8,128)(2,1)S(1)}, u32[]{:S(2)}, u32[]{:S(2)}) collective-permute-start(f16[4,128,256]{2,1,0:T(8,128)(2,1)S(1)} %bitcast.46), channel_id=1, source_target_pairs={{0,8},{8,0},{16,24},{24,16},{1,9},{9,1},{17,25},{25,17},{2,10},{10... | collective-permute-start | bytes 786440 | tf_op jit(solution)/shard_map/ppermute | solution.py:246
  58.9 6.3 %collective-permute-start.12 = (f16[2,128,256]{2,1,0:T(8,128)(2,1)S(1)}, f16[2,128,256]{2,1,0:T(8,128)(2,1)S(1)}, u32[]{:S(2)}, u32[]{:S(2)}) collective-permute-start(f16[2,128,256]{2,1,0:T(8,128)(2,1)S(1)} %pad_maximum_fusion.3), channel_id=1, source_target_pairs={{0,2},{1,3},{2,0},{3,1},{4,6},{5,7},{6,4},{7,5},{8,10},{9,11},{10,... | collective-permute-start | bytes 393224 | tf_op jit(solution)/shard_map/ppermute | solution.py:246
  60.5 6.6 %collective-permute-start.13 = (f16[2,128,256]{2,1,0:T(8,128)(2,1)S(1)}, f16[2,128,256]{2,1,0:T(8,128)(2,1)S(1)}, u32[]{:S(2)}, u32[]{:S(2)}) collective-permute-start(f16[2,128,256]{2,1,0:T(8,128)(2,1)S(1)} %pad_maximum_fusion.4), channel_id=1, source_target_pairs={{0,3},{1,2},{2,1},{3,0},{4,7},{5,6},{6,5},{7,4},{8,11},{9,10},{10,... | collective-permute-start | bytes 393224 | tf_op jit(solution)/shard_map/ppermute | solution.py:246
  60.7 13.2 %collective-permute-start.10 = (f16[2,128,256]{2,1,0:T(8,128)(2,1)S(1)}, f16[2,128,256]{2,1,0:T(8,128)(2,1)}, u32[]{:S(2)}, u32[]{:S(2)}) collective-permute-start(f16[2,128,256]{2,1,0:T(8,128)(2,1)S(1)} %pad_maximum_fusion.1), channel_id=1, source_target_pairs={{0,2},{1,3},{2,0},{3,1},{4,6},{5,7},{6,4},{7,5},{8,10},{9,11},{10,... | collective-permute-start | bytes 393224 | tf_op jit(solution)/shard_map/ppermute | solution.py:246
  63.0 11.0 %collective-permute-start.11 = (f16[2,128,256]{2,1,0:T(8,128)(2,1)}, f16[2,128,256]{2,1,0:T(8,128)(2,1)}, u32[]{:S(2)}, u32[]{:S(2)}) collective-permute-start(f16[2,128,256]{2,1,0:T(8,128)(2,1)} %pad_maximum_fusion.2), channel_id=1, source_target_pairs={{0,3},{1,2},{2,1},{3,0},{4,7},{5,6},{6,5},{7,4},{8,11},{9,10},{10,... | collective-permute-start | bytes 393224 | tf_op jit(solution)/shard_map/ppermute | solution.py:246
  63.5 1.6 %collective-permute-start.9 = (f16[4,128,256]{2,1,0:T(8,128)(2,1)S(1)}, f16[4,128,256]{2,1,0:T(8,128)(2,1)S(1)}, u32[]{:S(2)}, u32[]{:S(2)}) collective-permute-start(f16[4,128,256]{2,1,0:T(8,128)(2,1)S(1)} %pad_maximum_fusion), channel_id=1, source_target_pairs={{0,1},{1,0},{2,3},{3,2},{4,5},{5,4},{6,7},{7,6},{8,9},{9,8},{10,11... | collective-permute-start | bytes 786440 | tf_op jit(solution)/shard_map/ppermute | solution.py:246
  67.3 2.6 %copy-start.3 = (f32[2048,256]{1,0:T(8,128)S(1)}, f32[2048,256]{1,0:T(8,128)}, u32[]{:S(2)}) copy-start(f32[2048,256]{1,0:T(8,128)} %average_ref.1) | copy-start | bytes 6291460
  69.9 5.4 %copy-start.1 = (f32[512,1024]{1,0:T(8,128)S(1)}, f32[512,1024]{1,0:T(8,128)}, u32[]{:S(2)}) copy-start(f32[512,1024]{1,0:T(8,128)} %refs_1_.5) | copy-start | bytes 6291460
  69.9 5.4 %copy-start.2 = (f32[512,1024]{1,0:T(8,128)S(1)}, f32[512,1024]{1,0:T(8,128)}, u32[]{:S(2)}) copy-start(f32[512,1024]{1,0:T(8,128)} %refs_2_.5) | copy-start | bytes 6291460
  73.9 1.7 %copy-start = (f32[512,1024]{1,0:T(8,128)S(1)}, f32[512,1024]{1,0:T(8,128)}, u32[]{:S(2)}) copy-start(f32[512,1024]{1,0:T(8,128)} %refs_0_.5) | copy-start | bytes 6291460
  73.9 1.7 %copy-start.5 = (f32[4,256]{1,0:T(4,128)S(1)}, f32[4,256]{1,0:T(4,128)}, u32[]{:S(2)}) copy-start(f32[4,256]{1,0:T(4,128)} %refs_4_.1) | copy-start | bytes 12292
  73.9 1.7 %copy-start.6 = (f32[4,256]{1,0:T(4,128)S(1)}, f32[4,256]{1,0:T(4,128)}, u32[]{:S(2)}) copy-start(f32[4,256]{1,0:T(4,128)} %refs_5_.1) | copy-start | bytes 12292
  73.9 1.7 %copy-start.7 = (f32[4,256]{1,0:T(4,128)S(1)}, f32[4,256]{1,0:T(4,128)}, u32[]{:S(2)}) copy-start(f32[4,256]{1,0:T(4,128)} %refs_6_.1) | copy-start | bytes 12292
  73.9 1.7 %copy-start.8 = (f32[4,256]{1,0:T(4,128)S(1)}, f32[4,256]{1,0:T(4,128)}, u32[]{:S(2)}) copy-start(f32[4,256]{1,0:T(4,128)} %refs_7_.1) | copy-start | bytes 12292

commit v2 on v1

--- a/solution.py
+++ b/solution.py
@@ -187,40 +187,46 @@
 def block_average(place, norm, gradient, states, average):
     groups, cols, rows, width = gradient.shape
     span = groups * rows
+    pair = 2
 
     def body(
         place_ref, norm_ref, gradient_ref, states_ref, average_ref, out_ref, passed_ref
     ):
         passed_ref[...] = norm_ref[...]
         clip_scale = clip_of(norm_ref)
-        for group in range(groups):
-            here = slice(group * rows, (group + 1) * rows)
-            master, first, second = (states_ref[0, i, here] for i in range(3))
-            master_new, _, _ = adam_step(
-                gradient_ref[place_ref[0] ^ group, 0],
-                clip_scale,
-                first,
-                second,
-                master,
-                decay_rate,
-            )
-            out_ref[here] = (
-                ema_keep * average_ref[here] + (1.0 - ema_keep) * master_new
-            )
-
-    block = pl.BlockSpec((span, width), lambda c, place: (c, 0))
+        for own in range(pair):
+            other = (place_ref[1] ^ own) & (pair - 1)
+            for group in range(groups):
+                rows_here = slice(group * rows, (group + 1) * rows)
+                here = slice(own * span + group * rows, own * span + (group + 1) * rows)
+                master, first, second = (
+                    states_ref[own, i, rows_here] for i in range(3)
+                )
+                master_new, _, _ = adam_step(
+                    gradient_ref[place_ref[0] ^ group, other],
+                    clip_scale,
+                    first,
+                    second,
+                    master,
+                    decay_rate,
+                )
+                out_ref[here] = (
+                    ema_keep * average_ref[here] + (1.0 - ema_keep) * master_new
+                )
+
+    block = pl.BlockSpec((pair * span, width), lambda c, place: (c, 0))
     return pl.pallas_call(
         body,
         grid_spec=pltpu.PrefetchScalarGridSpec(
             num_scalar_prefetch=1,
-            grid=(cols,),
+            grid=(cols // pair,),
             in_specs=[
                 pl.BlockSpec(norm.shape, lambda c, place: (0, 0)),
                 pl.BlockSpec(
-                    (groups, 1, rows, width),
-                    lambda c, place: (0, place[1] ^ c, 0, 0),
+                    (groups, pair, rows, width),
+                    lambda c, place: (0, (place[1] >> 1) ^ c, 0, 0),
                 ),
-                pl.BlockSpec((1, 3, span, width), lambda c, place: (c, 0, 0, 0)),
+                pl.BlockSpec((pair, 3, span, width), lambda c, place: (c, 0, 0, 0)),
                 block,
             ],
             out_specs=[block, pl.BlockSpec(norm.shape, lambda c, place: (0, 0))],
@@ -228,7 +234,7 @@
         out_shape=[
             jax.ShapeDtypeStruct(x.shape, x.dtype) for x in (average, norm)
         ],
-        compiler_params=pltpu.CompilerParams(vmem_limit_bytes=16 * 2**20),
+        compiler_params=pltpu.CompilerParams(vmem_limit_bytes=24 * 2**20),
         name="block_average",
     )(place, norm, gradient, states, average)
 

time: 81.5 us -> 81.3 us (level)
  no operation moved by 1% of the time
where the time goes in v2:
time: 81.3 us; the launch traced here: 80.7 us
  starting transfers between devices  25.3 us (31%)
  blocking collectives  17.6 us (22%)
  Pallas kernels  13.9 us (17%)
  waiting for transfers between devices  12.2 us (15%)
  other arithmetic  8.2 us (10%)
  local copies, waits for them, and re-layouts  2.56 us (3%)
  between operations  0.89 us (1%)
    ppermute x14, starting transfers between devices, send(): return lax.ppermute(held, axis, [(i, i ^ s) for i in range(size)])  20.6 us
    all_gather x1, blocking collectives, shards(): norm = lax.all_gather(hand_on(norm), ('row', 'col'), tiled=True)  17.6 us
    ppermute x14, waiting for transfers between devices, send(): return lax.ppermute(held, axis, [(i, i ^ s) for i in range(size)])  12.2 us
    pallas_call x2, Pallas kernels, flat_update(): pl.pallas_call(body, grid_spec=pltpu.PrefetchScalarGridSpec(num_scalar_pr...  5.29 us
    all_to_all x1, starting transfers between devices, shards(): lax.all_to_all(by_column(states, cols, after).astype(f16), 'col', split_a...  4.66 us
    pallas_call x1, Pallas kernels, block_average(): pl.pallas_call(body, grid_spec=pltpu.PrefetchScalarGridSpec(num_scalar_pr...  3.73 us
    pallas_call x1, Pallas kernels, by_column(): pl.pallas_call(body, grid=(cols,), in_specs=[pl.BlockSpec((rows, width),...  3.55 us
    convert_element_type x1, other arithmetic, shards(): block_states.astype(f32)  2.59 us
  transfers between devices with their start and end apart: 15, of which 4 were waited for; matrix products, arithmetic and copies ran while one was open for 9% of the time, Pallas kernels for 11%

profile of v2, /device:TPU:0, one launch (start us, length us, event | category | flops | bytes accessed | tf_op | source)
XLA Modules:
  0.0 80.7 jit_solution(13420031747285453649)
XLA Ops:
  0.6 1.2 %copy-done.4 = bf16[1,2048,256]{2,1,0:T(8,128)(2,1)S(1)} copy-done((bf16[1,2048,256]{2,1,0:T(8,128)(2,1)S(1)}, bf16[1,2048,256]{2,1,0:T(8,128)(2,1)}, u32[]{:S(2)}) %copy-start.4) | copy-done | bytes 1048600
  1.9 0.7 copy-done.9
  2.5 0.1 arrange.1
  2.6 3.1 %collective-permute-start = (bf16[528,256]{1,0:T(8,128)(2,1)S(1)}, bf16[528,256]{1,0:T(8,128)(2,1)S(1)}, u32[]{:S(2)}, u32[]{:S(2)}) collective-permute-start(bf16[528,256]{1,0:T(8,128)(2,1)S(1)} %get-tuple-element.27), channel_id=1, source_target_pairs={{0,8},{8,0},{16,24},{24,16},{1,9},{9,1},{17,25},{25,17},{2,10},{10... | collective-permute-start | bytes 811016 | tf_op jit(solution)/shard_map/ppermute | solution.py:252
  5.7 2.6 %collective-permute-start.1 = (bf16[528,256]{1,0:T(8,128)(2,1)S(1)}, bf16[528,256]{1,0:T(8,128)(2,1)S(1)}, u32[]{:S(2)}, u32[]{:S(2)}) collective-permute-start(bf16[528,256]{1,0:T(8,128)(2,1)S(1)} %get-tuple-element.28), channel_id=1, source_target_pairs={{0,16},{8,24},{16,0},{24,8},{1,17},{9,25},{17,1},{25,9},{2,18},{10... | collective-permute-start | bytes 811016 | tf_op jit(solution)/shard_map/ppermute | solution.py:252
  8.3 3.5 %by_column.1 = f32[4,3,512,256]{3,2,1,0:T(8,128)S(1)} custom-call(f32[512,1024]{1,0:T(8,128)} %refs_0_.5, f32[512,1024]{1,0:T(8,128)} %refs_1_.5, f32[512,1024]{1,0:T(8,128)} %refs_2_.5, f32[8,128]{1,0:T(8,128)S(1)} %get-tuple-element.30.refs_3_), custom_call_target="tpu_custom_call" | custom-call | tf_op jit(solution)/shard_map/by_column/pallas_call | solution.py:88
  11.9 2.1 %convert_element_type.51 = f16[4,3,512,256]{3,2,1,0:T(8,128)(2,1)} convert(f32[4,3,512,256]{3,2,1,0:T(8,128)S(1)} %by_column.1) | non-fusion elementwise | flops 1572864 | bytes 9437184 | tf_op jit(solution)/shard_map/convert_element_type | solution.py:287
  14.0 4.7 %all-to-all-start = ((f16[4,3,512,256]{3,2,1,0:T(8,128)(2,1)}), f16[4,3,512,256]{3,2,1,0:T(8,128)(2,1)}, u32[]{:S(2)}, u32[]{:S(2)}) async-start(f16[4,3,512,256]{3,2,1,0:T(8,128)(2,1)} %convert_element_type.51), calls=%async_computation | async-start | bytes 6291456 | tf_op jit(solution)/shard_map/all_to_all | solution.py:286
  18.6 0.1 pad_add_fusion.place_ref
  18.7 0.0 collective-permute-done
  18.7 8.9 %collective-permute-done.1 = bf16[528,256]{1,0:T(8,128)(2,1)S(1)} collective-permute-done((bf16[528,256]{1,0:T(8,128)(2,1)S(1)}, bf16[528,256]{1,0:T(8,128)(2,1)S(1)}, u32[]{:S(2)}, u32[]{:S(2)}) %collective-permute-start.1) | collective-permute-done | bytes 270368 | tf_op jit(solution)/shard_map/ppermute | solution.py:252
  27.6 0.1 add_add_fusion
  27.8 0.1 slice_convert_fusion
  27.9 2.5 %collective-permute-start.5 = (f32[1,256]{1,0:T(1,128)S(1)}, f32[1,256]{1,0:T(1,128)S(1)}, u32[]{:S(2)}, u32[]{:S(2)}) collective-permute-start(f32[1,256]{1,0:T(1,128)S(1)} %bitcast.53), channel_id=1, source_target_pairs={{0,24},{8,16},{16,8},{24,0},{1,25},{9,17},{17,9},{25,1},{2,26},{10... | collective-permute-start | bytes 3080 | tf_op jit(solution)/shard_map/ppermute | solution.py:252
  30.4 3.9 %collective-permute-start.4 = (f32[1,256]{1,0:T(1,128)S(1)}, f32[1,256]{1,0:T(1,128)S(1)}, u32[]{:S(2)}, u32[]{:S(2)}) collective-permute-start(f32[1,256]{1,0:T(1,128)S(1)} %bitcast.54), channel_id=1, source_target_pairs={{0,16},{8,24},{16,0},{24,8},{1,17},{9,25},{17,1},{25,9},{2,18},{10... | collective-permute-start | bytes 3080 | tf_op jit(solution)/shard_map/ppermute | solution.py:252
  34.3 0.1 collective-permute-start.3
  34.4 2.4 %collective-permute-start.8 = (f16[4,128,256]{2,1,0:T(8,128)(2,1)S(1)}, f16[4,128,256]{2,1,0:T(8,128)(2,1)S(1)}, u32[]{:S(2)}, u32[]{:S(2)}) collective-permute-start(f16[4,128,256]{2,1,0:T(8,128)(2,1)S(1)} %bitcast.44), channel_id=1, source_target_pairs={{0,24},{8,16},{16,8},{24,0},{1,25},{9,17},{17,9},{25,1},{2,26},{10... | collective-permute-start | bytes 786440 | tf_op jit(solution)/shard_map/ppermute | solution.py:252
  36.9 1.1 %collective-permute-start.7 = (f16[4,128,256]{2,1,0:T(8,128)(2,1)S(1)}, f16[4,128,256]{2,1,0:T(8,128)(2,1)S(1)}, u32[]{:S(2)}, u32[]{:S(2)}) collective-permute-start(f16[4,128,256]{2,1,0:T(8,128)(2,1)S(1)} %bitcast.45), channel_id=1, source_target_pairs={{0,16},{8,24},{16,0},{24,8},{1,17},{9,25},{17,1},{25,9},{2,18},{10... | collective-permute-start | bytes 786440 | tf_op jit(solution)/shard_map/ppermute | solution.py:252
  37.9 0.0 collective-permute-done.5
  37.9 1.0 %collective-permute-start.6 = (f16[4,128,256]{2,1,0:T(8,128)(2,1)S(1)}, f16[4,128,256]{2,1,0:T(8,128)(2,1)S(1)}, u32[]{:S(2)}, u32[]{:S(2)}) collective-permute-start(f16[4,128,256]{2,1,0:T(8,128)(2,1)S(1)} %bitcast.46), channel_id=1, source_target_pairs={{0,8},{8,0},{16,24},{24,16},{1,9},{9,1},{17,25},{25,17},{2,10},{10... | collective-permute-start | bytes 786440 | tf_op jit(solution)/shard_map/ppermute | solution.py:252
  39.0 0.6 add_add_fusion.1.norm_ref
  39.5 1.2 %hand_on.1 = f32[1,256]{1,0:T(1,128)} custom-call(f32[1,256]{1,0:T(1,128)} %add_add_fusion.1.norm_ref), custom_call_target="tpu_custom_call" | custom-call | bytes 60000000 | tf_op jit(solution)/shard_map/hand_on/pallas_call | solution.py:104
  40.8 17.6 %all-gather = f32[8,1,256]{2,1,0:T(1,128)S(1)} all-gather(f32[1,1,256]{2,1,0:T(1,128)} %bitcast.57), channel_id=1, replica_groups=mesh['dp'=4,'row'=2,'col'=4] {'row','col'}, dimensions={0}, use_global_device_ids=true | all-gather | bytes 9216 | tf_op jit(solution)/shard_map/all_gather | solution.py:302
  58.5 0.3 collective-permute-done.7
  58.9 1.6 %collective-permute-start.12 = (f16[2,128,256]{2,1,0:T(8,128)(2,1)S(1)}, f16[2,128,256]{2,1,0:T(8,128)(2,1)S(1)}, u32[]{:S(2)}, u32[]{:S(2)}) collective-permute-start(f16[2,128,256]{2,1,0:T(8,128)(2,1)S(1)} %pad_maximum_fusion.3), channel_id=1, source_target_pairs={{0,2},{1,3},{2,0},{3,1},{4,6},{5,7},{6,4},{7,5},{8,10},{9,11},{10,... | collective-permute-start | bytes 393224 | tf_op jit(solution)/shard_map/ppermute | solution.py:252
  60.5 0.1 collective-permute-start.13
  60.6 0.1 fusion.3
  60.7 1.6 %collective-permute-start.10 = (f16[2,128,256]{2,1,0:T(8,128)(2,1)S(1)}, f16[2,128,256]{2,1,0:T(8,128)(2,1)}, u32[]{:S(2)}, u32[]{:S(2)}) collective-permute-start(f16[2,128,256]{2,1,0:T(8,128)(2,1)S(1)} %pad_maximum_fusion.1), channel_id=1, source_target_pairs={{0,2},{1,3},{2,0},{3,1},{4,6},{5,7},{6,4},{7,5},{8,10},{9,11},{10,... | collective-permute-start | bytes 393224 | tf_op jit(solution)/shard_map/ppermute | solution.py:252
  62.3 0.7 pad_maximum_fusion.2
  63.0 0.5 collective-permute-start.11
  63.4 0.1 pad_maximum_fusion
  63.5 0.2 collective-permute-start.9
  63.8 0.3 maximum_convert_fusion.gradient_ref
  64.1 1.0 %collective-permute-done.9 = f16[4,128,256]{2,1,0:T(8,128)(2,1)S(1)} collective-permute-done((f16[4,128,256]{2,1,0:T(8,128)(2,1)S(1)}, f16[4,128,256]{2,1,0:T(8,128)(2,1)S(1)}, u32[]{:S(2)}, u32[]{:S(2)}) %collective-permute-start.9) | collective-permute-done | bytes 262176 | tf_op jit(solution)/shard_map/ppermute | solution.py:252
  65.2 0.0 collective-permute-done.12
  65.2 2.0 %collective-permute-done.13 = f16[2,128,256]{2,1,0:T(8,128)(2,1)S(1)} collective-permute-done((f16[2,128,256]{2,1,0:T(8,128)(2,1)S(1)}, f16[2,128,256]{2,1,0:T(8,128)(2,1)S(1)}, u32[]{:S(2)}, u32[]{:S(2)}) %collective-permute-start.13) | collective-permute-done | bytes 131104 | tf_op jit(solution)/shard_map/ppermute | solution.py:252
  67.1 0.1 maximum_convert_fusion.1.gradient_ref
  67.3 0.0 copy-start.3
  67.3 2.6 %convert_element_type.52.states_ref = f32[4,3,512,256]{3,2,1,0:T(8,128)S(1)} convert(f16[4,3,512,256]{3,2,1,0:T(8,128)(2,1)} %all-to-all-done) | non-fusion elementwise | flops 1572864 | bytes 9437184 | tf_op jit(solution)/shard_map/convert_element_type | solution.py:315
  69.9 0.0 copy-start.1
  69.9 0.0 copy-start.2
  69.9 3.7 %block_average.1 = (f32[2048,256]{1,0:T(8,128)}, f32[8,256]{1,0:T(8,128)S(1)}) custom-call(s32[2]{0:T(128)S(1)} %pad_add_fusion.place_ref, f32[8,256]{1,0:T(8,128)S(1)} %bitcast.42, f32[4,4,128,256]{3,2,1,0:T(8,128)S(1)} %maximum_convert_fusion.gradient_ref, f32[4,3,512,256]{3,2,1,0:T(8,128)S(1)} %convert_element_type.52.states_ref, f32[2048,256]{1,0:T(8,128)S(1)} %copy-done.3), custom_call_target="tpu_custom_call" | custom-call | tf_op jit(solution)/shard_map/block_average/pallas_call | solution.py:218
  73.7 0.0 copy-start.8
  73.7 1.3 %convert_add_fusion = f32[2,4,128,256]{3,2,0,1:T(8,128)S(1)} fusion(f16[2,1,128,256]{3,2,0,1:T(8,128)(2,1)} %bitcast.18, f16[2,1,128,256]{3,2,0,1:T(8,128)(2,1)} %bitcast.16, f16[2,1,128,256]{3,2,0,1:T(8,128)(2,1)S(1)} %get-tuple-element.57, f16[2,1,128,256]{3,2,0,1:T(8,128)(2,1)S(1)} %maximum_bitcast_fusion, f32[256]{0:T(256)S(1)} %bitcast.58), kind=kLoop, calls=%fused_computation.1 | loop fusion | flops 1310720 | bytes 1573888 | tf_op jit(solution)/shard_map/add | solution.py:321
  75.0 0.1 copy.25.gradient_ref
  75.1 0.3 copy-done
  75.4 2.8 %flat_update.2 = (f32[512,1024]{1,0:T(8,128)}, f32[512,1024]{1,0:T(8,128)}, f32[512,1024]{1,0:T(8,128)}, f32[8,256]{1,0:T(8,128)S(1)}, f32[4,256]{1,0:T(4,128)},...) custom-call(s32[2]{0:T(128)S(1)} %pad_add_fusion.place_ref, f32[8,256]{1,0:T(8,128)S(1)} %get-tuple-element.32.norm_ref, ...), custom_call_target="tpu_custom_call" | custom-call | tf_op jit(solution)/shard_map/flat_update/pallas_call | solution.py:162
  78.2 2.5 %flat_update.3 = (f32[512,1024]{1,0:T(8,128)}, f32[512,1024]{1,0:T(8,128)}, f32[512,1024]{1,0:T(8,128)}, f32[8,256]{1,0:T(8,128)}) custom-call(s32[2]{0:T(128)S(1)} %pad_add_fusion.place_ref, f32[8,256]{1,0:T(8,128)S(1)} %get-tuple-element.33.norm_ref, ...), custom_call_target="tpu_custom_call", output_to_operand_aliasing={{0}: (6, {}), {1}: (7, {}), {2}: (8, {})} | custom-call | tf_op jit(solution)/shard_map/flat_update/pallas_call | solution.py:162
  (35 shorter events, 0.4 us)
Async XLA Ops:
  0.6 1.2 %copy-start.4 = (bf16[1,2048,256]{2,1,0:T(8,128)(2,1)S(1)}, bf16[1,2048,256]{2,1,0:T(8,128)(2,1)}, u32[]{:S(2)}) copy-start(bf16[1,2048,256]{2,1,0:T(8,128)(2,1)} %param.10) | copy-start | bytes 3145732
  1.9 0.7 copy-start.9
  2.6 16.1 %collective-permute-start = (bf16[528,256]{1,0:T(8,128)(2,1)S(1)}, bf16[528,256]{1,0:T(8,128)(2,1)S(1)}, u32[]{:S(2)}, u32[]{:S(2)}) collective-permute-start(bf16[528,256]{1,0:T(8,128)(2,1)S(1)} %get-tuple-element.27), channel_id=1, source_target_pairs={{0,8},{8,0},{16,24},{24,16},{1,9},{9,1},{17,25},{25,17},{2,10},{10... | collective-permute-start | bytes 811016 | tf_op jit(solution)/shard_map/ppermute | solution.py:252
  5.7 21.9 %collective-permute-start.1 = (bf16[528,256]{1,0:T(8,128)(2,1)S(1)}, bf16[528,256]{1,0:T(8,128)(2,1)S(1)}, u32[]{:S(2)}, u32[]{:S(2)}) collective-permute-start(bf16[528,256]{1,0:T(8,128)(2,1)S(1)} %get-tuple-element.28), channel_id=1, source_target_pairs={{0,16},{8,24},{16,0},{24,8},{1,17},{9,25},{17,1},{25,9},{2,18},{10... | collective-permute-start | bytes 811016 | tf_op jit(solution)/shard_map/ppermute | solution.py:252
  8.3 19.3 %collective-permute-start.2 = (bf16[528,256]{1,0:T(8,128)(2,1)S(1)}, bf16[528,256]{1,0:T(8,128)(2,1)S(1)}, u32[]{:S(2)}, u32[]{:S(2)}) collective-permute-start(bf16[528,256]{1,0:T(8,128)(2,1)S(1)} %get-tuple-element.29), channel_id=1, source_target_pairs={{0,24},{8,16},{16,8},{24,0},{1,25},{9,17},{17,9},{25,1},{2,26},{10... | collective-permute-start | bytes 811016 | tf_op jit(solution)/shard_map/ppermute | solution.py:252
  14.0 53.3 %all-to-all-start = ((f16[4,3,512,256]{3,2,1,0:T(8,128)(2,1)}), f16[4,3,512,256]{3,2,1,0:T(8,128)(2,1)}, u32[]{:S(2)}, u32[]{:S(2)}) async-start(f16[4,3,512,256]{3,2,1,0:T(8,128)(2,1)} %convert_element_type.51), calls=%async_computation | async-start | bytes 6291456 | tf_op jit(solution)/shard_map/all_to_all | solution.py:286
  27.9 10.1 %collective-permute-start.5 = (f32[1,256]{1,0:T(1,128)S(1)}, f32[1,256]{1,0:T(1,128)S(1)}, u32[]{:S(2)}, u32[]{:S(2)}) collective-permute-start(f32[1,256]{1,0:T(1,128)S(1)} %bitcast.53), channel_id=1, source_target_pairs={{0,24},{8,16},{16,8},{24,0},{1,25},{9,17},{17,9},{25,1},{2,26},{10... | collective-permute-start | bytes 3080 | tf_op jit(solution)/shard_map/ppermute | solution.py:252
  30.4 8.6 %collective-permute-start.4 = (f32[1,256]{1,0:T(1,128)S(1)}, f32[1,256]{1,0:T(1,128)S(1)}, u32[]{:S(2)}, u32[]{:S(2)}) collective-permute-start(f32[1,256]{1,0:T(1,128)S(1)} %bitcast.54), channel_id=1, source_target_pairs={{0,16},{8,24},{16,0},{24,8},{1,17},{9,25},{17,1},{25,9},{2,18},{10... | collective-permute-start | bytes 3080 | tf_op jit(solution)/shard_map/ppermute | solution.py:252
  34.3 4.6 %collective-permute-start.3 = (f32[1,256]{1,0:T(1,128)S(1)}, f32[1,256]{1,0:T(1,128)S(1)}, u32[]{:S(2)}, u32[]{:S(2)}) collective-permute-start(f32[1,256]{1,0:T(1,128)S(1)} %bitcast.55), channel_id=1, source_target_pairs={{0,8},{8,0},{16,24},{24,16},{1,9},{9,1},{17,25},{25,17},{2,10},{10... | collective-permute-start | bytes 3080 | tf_op jit(solution)/shard_map/ppermute | solution.py:252
  34.4 24.0 %collective-permute-start.8 = (f16[4,128,256]{2,1,0:T(8,128)(2,1)S(1)}, f16[4,128,256]{2,1,0:T(8,128)(2,1)S(1)}, u32[]{:S(2)}, u32[]{:S(2)}) collective-permute-start(f16[4,128,256]{2,1,0:T(8,128)(2,1)S(1)} %bitcast.44), channel_id=1, source_target_pairs={{0,24},{8,16},{16,8},{24,0},{1,25},{9,17},{17,9},{25,1},{2,26},{10... | collective-permute-start | bytes 786440 | tf_op jit(solution)/shard_map/ppermute | solution.py:252
  36.9 22.0 %collective-permute-start.7 = (f16[4,128,256]{2,1,0:T(8,128)(2,1)S(1)}, f16[4,128,256]{2,1,0:T(8,128)(2,1)S(1)}, u32[]{:S(2)}, u32[]{:S(2)}) collective-permute-start(f16[4,128,256]{2,1,0:T(8,128)(2,1)S(1)} %bitcast.45), channel_id=1, source_target_pairs={{0,16},{8,24},{16,0},{24,8},{1,17},{9,25},{17,1},{25,9},{2,18},{10... | collective-permute-start | bytes 786440 | tf_op jit(solution)/shard_map/ppermute | solution.py:252
  37.9 22.7 %collective-permute-start.6 = (f16[4,128,256]{2,1,0:T(8,128)(2,1)S(1)}, f16[4,128,256]{2,1,0:T(8,128)(2,1)S(1)}, u32[]{:S(2)}, u32[]{:S(2)}) collective-permute-start(f16[4,128,256]{2,1,0:T(8,128)(2,1)S(1)} %bitcast.46), channel_id=1, source_target_pairs={{0,8},{8,0},{16,24},{24,16},{1,9},{9,1},{17,25},{25,17},{2,10},{10... | collective-permute-start | bytes 786440 | tf_op jit(solution)/shard_map/ppermute | solution.py:252
  58.9 6.3 %collective-permute-start.12 = (f16[2,128,256]{2,1,0:T(8,128)(2,1)S(1)}, f16[2,128,256]{2,1,0:T(8,128)(2,1)S(1)}, u32[]{:S(2)}, u32[]{:S(2)}) collective-permute-start(f16[2,128,256]{2,1,0:T(8,128)(2,1)S(1)} %pad_maximum_fusion.3), channel_id=1, source_target_pairs={{0,2},{1,3},{2,0},{3,1},{4,6},{5,7},{6,4},{7,5},{8,10},{9,11},{10,... | collective-permute-start | bytes 393224 | tf_op jit(solution)/shard_map/ppermute | solution.py:252
  60.5 6.6 %collective-permute-start.13 = (f16[2,128,256]{2,1,0:T(8,128)(2,1)S(1)}, f16[2,128,256]{2,1,0:T(8,128)(2,1)S(1)}, u32[]{:S(2)}, u32[]{:S(2)}) collective-permute-start(f16[2,128,256]{2,1,0:T(8,128)(2,1)S(1)} %pad_maximum_fusion.4), channel_id=1, source_target_pairs={{0,3},{1,2},{2,1},{3,0},{4,7},{5,6},{6,5},{7,4},{8,11},{9,10},{10,... | collective-permute-start | bytes 393224 | tf_op jit(solution)/shard_map/ppermute | solution.py:252
  60.7 13.0 %collective-permute-start.10 = (f16[2,128,256]{2,1,0:T(8,128)(2,1)S(1)}, f16[2,128,256]{2,1,0:T(8,128)(2,1)}, u32[]{:S(2)}, u32[]{:S(2)}) collective-permute-start(f16[2,128,256]{2,1,0:T(8,128)(2,1)S(1)} %pad_maximum_fusion.1), channel_id=1, source_target_pairs={{0,2},{1,3},{2,0},{3,1},{4,6},{5,7},{6,4},{7,5},{8,10},{9,11},{10,... | collective-permute-start | bytes 393224 | tf_op jit(solution)/shard_map/ppermute | solution.py:252
  63.0 10.7 %collective-permute-start.11 = (f16[2,128,256]{2,1,0:T(8,128)(2,1)}, f16[2,128,256]{2,1,0:T(8,128)(2,1)}, u32[]{:S(2)}, u32[]{:S(2)}) collective-permute-start(f16[2,128,256]{2,1,0:T(8,128)(2,1)} %pad_maximum_fusion.2), channel_id=1, source_target_pairs={{0,3},{1,2},{2,1},{3,0},{4,7},{5,6},{6,5},{7,4},{8,11},{9,10},{10,... | collective-permute-start | bytes 393224 | tf_op jit(solution)/shard_map/ppermute | solution.py:252
  63.5 1.6 %collective-permute-start.9 = (f16[4,128,256]{2,1,0:T(8,128)(2,1)S(1)}, f16[4,128,256]{2,1,0:T(8,128)(2,1)S(1)}, u32[]{:S(2)}, u32[]{:S(2)}) collective-permute-start(f16[4,128,256]{2,1,0:T(8,128)(2,1)S(1)} %pad_maximum_fusion), channel_id=1, source_target_pairs={{0,1},{1,0},{2,3},{3,2},{4,5},{5,4},{6,7},{7,6},{8,9},{9,8},{10,11... | collective-permute-start | bytes 786440 | tf_op jit(solution)/shard_map/ppermute | solution.py:252
  67.3 2.6 %copy-start.3 = (f32[2048,256]{1,0:T(8,128)S(1)}, f32[2048,256]{1,0:T(8,128)}, u32[]{:S(2)}) copy-start(f32[2048,256]{1,0:T(8,128)} %average_ref.1) | copy-start | bytes 6291460
  69.9 5.2 %copy-start.1 = (f32[512,1024]{1,0:T(8,128)S(1)}, f32[512,1024]{1,0:T(8,128)}, u32[]{:S(2)}) copy-start(f32[512,1024]{1,0:T(8,128)} %refs_1_.5) | copy-start | bytes 6291460
  69.9 5.2 %copy-start.2 = (f32[512,1024]{1,0:T(8,128)S(1)}, f32[512,1024]{1,0:T(8,128)}, u32[]{:S(2)}) copy-start(f32[512,1024]{1,0:T(8,128)} %refs_2_.5) | copy-start | bytes 6291460
  73.7 1.7 %copy-start = (f32[512,1024]{1,0:T(8,128)S(1)}, f32[512,1024]{1,0:T(8,128)}, u32[]{:S(2)}) copy-start(f32[512,1024]{1,0:T(8,128)} %refs_0_.5) | copy-start | bytes 6291460
  73.7 1.7 %copy-start.5 = (f32[4,256]{1,0:T(4,128)S(1)}, f32[4,256]{1,0:T(4,128)}, u32[]{:S(2)}) copy-start(f32[4,256]{1,0:T(4,128)} %refs_4_.1) | copy-start | bytes 12292
  73.7 1.7 %copy-start.6 = (f32[4,256]{1,0:T(4,128)S(1)}, f32[4,256]{1,0:T(4,128)}, u32[]{:S(2)}) copy-start(f32[4,256]{1,0:T(4,128)} %refs_5_.1) | copy-start | bytes 12292
  73.7 1.7 %copy-start.7 = (f32[4,256]{1,0:T(4,128)S(1)}, f32[4,256]{1,0:T(4,128)}, u32[]{:S(2)}) copy-start(f32[4,256]{1,0:T(4,128)} %refs_6_.1) | copy-start | bytes 12292
  73.7 1.7 %copy-start.8 = (f32[4,256]{1,0:T(4,128)S(1)}, f32[4,256]{1,0:T(4,128)}, u32[]{:S(2)}) copy-start(f32[4,256]{1,0:T(4,128)} %refs_7_.1) | copy-start | bytes 12292
